TPU v7x, 128 devices: a whole 4x4x4 slice. The times are simulated.
128 devices in a mesh: dp: 16 (over z, y), tensor: 8 (over x, core).
Axes of the slice: x: 4, y: 4, z: 4, core: 2. Of those that a mesh axis runs over, the one named last changes fastest.
Arguments:
- tokens: bfloat16 [1024, 8192], P('tensor', 'dp'), may hold values from -6 to 6
- gate_int_codes: bfloat16 [8192, 26624], P('dp', 'tensor'), may hold values from -8 to 7, as said below
- up_int_codes: bfloat16 [8192, 26624], P('dp', 'tensor'), may hold values from -8 to 7, as said below
- down_int_codes: bfloat16 [26624, 8192], P('tensor', 'dp'), may hold values from -8 to 7, as said below
- gate_column_scale: float32 [26624], P('tensor'), may hold values from 0.0006629126 to 0.006629126
- up_column_scale: float32 [26624], P('tensor'), may hold values from 0.0006629126 to 0.006629126
- down_column_scale: float32 [8192], P('dp'), may hold values from 0.00036771776 to 0.0036771775
- row_adapter_index: int32 [1024], replicated, may hold values from 0 to 255
- adapter_shrink_weight: bfloat16 [256, 26624, 16], P('dp', 'tensor'), may hold values from -0.0390625 to 0.0390625
- adapter_expand_weight: bfloat16 [256, 16, 8192], P(None, None, 'dp'), may hold values from -1.5 to 1.5
Outputs:
- layer_out: bfloat16 [1024, 8192], P('tensor', 'dp')
Inputs may be any that keep to these rules, and one draw needn't show every extreme that they name: `gate_int_codes`: every entry is a whole number. `up_int_codes`: every entry is a whole number. `down_int_codes`: every entry is a whole number.
All inputs are finite; a program needn't handle non-finite values.
Results may differ from a plain program's by a relative error of at most 0.03.
Values may be sent and summed in bfloat16 or wider, within the bound.
A program may use at most 192 MiB of HBM per device.

v0:
```python
import math

import jax
import jax.numpy as jnp
from jax import lax
from jax.sharding import PartitionSpec as P

FACTOR = 13
ADAPTER_RANK = 16


def shortened(value):
    return jax.tree.map(lambda a: a.astype(jnp.bfloat16) if a.dtype == jnp.float32 else a, value)


def sylvester(mat_order):
    indices = jnp.arange(mat_order, dtype=jnp.int32)
    common = jnp.bitwise_and(indices[:, None], indices[None, :])
    parity = jnp.zeros((mat_order, mat_order), jnp.int32)
    for bit_pos in range(max(mat_order.bit_length() - 1, 0)):
        parity = parity + jnp.bitwise_and(jnp.right_shift(common, bit_pos), 1)
    parity = jnp.bitwise_and(parity, 1)
    return (1 - 2 * parity).astype(jnp.float32) / jnp.float32(math.sqrt(mat_order))


def hartley(mat_order):
    indices = jnp.arange(mat_order, dtype=jnp.int32)
    product = indices[:, None] * indices[None, :] % mat_order
    angles = product.astype(jnp.float32) * jnp.float32(2.0 * math.pi / mat_order)
    return (jnp.cos(angles) + jnp.sin(angles)) / jnp.float32(math.sqrt(mat_order))


def dequant(codes, scale):
    return (codes.astype(jnp.float32) * scale).astype(jnp.bfloat16)


def local_rotate(values):
    highest = lax.Precision.HIGHEST
    rows_here, columns = values.shape
    local_len = columns // FACTOR
    shaped = values.reshape(rows_here, FACTOR, local_len)
    shaped = jnp.einsum("rad,ed->rae", shaped, sylvester(local_len), precision=highest)
    shaped = jnp.einsum("rad,ba->rbd", shaped, hartley(FACTOR), precision=highest)
    return shaped.reshape(rows_here, columns)


def cross_rotate(values):
    highest = lax.Precision.HIGHEST
    n_tensor = lax.axis_size("tensor")
    rows_here, columns = values.shape
    signs = sylvester(n_tensor)
    mixed_vals = jnp.einsum(
        "rtc,st->rsc",
        lax.all_to_all(
            values.reshape(rows_here, 1, columns).astype(jnp.bfloat16),
            "tensor",
            split_axis=0,
            concat_axis=1,
            tiled=True,
        ).astype(jnp.float32),
        signs,
        precision=highest,
    )
    outcome = lax.all_to_all(
        shortened(mixed_vals), "tensor", split_axis=1, concat_axis=0, tiled=True
    ).astype(mixed_vals.dtype)
    return outcome.reshape(rows_here, columns)


def expanded_rows(shrunk_rows, selected_adapter_index, adapter_expand_weight):
    selected_rows = jnp.take(adapter_expand_weight, selected_adapter_index, axis=0)
    return jnp.einsum(
        "rk,rkd->rd",
        shrunk_rows,
        selected_rows.astype(jnp.float32),
        precision=lax.Precision.HIGHEST,
    )


def body(
    tokens,
    gate_int_codes,
    up_int_codes,
    down_int_codes,
    gate_column_scale,
    up_column_scale,
    down_column_scale,
    row_adapter_index,
    adapter_shrink_weight,
    adapter_expand_weight,
):
    total_rows = row_adapter_index.shape[0]
    hidden_columns = gate_int_codes.shape[1]
    model_cols = down_int_codes.shape[1]
    present_adapters = adapter_shrink_weight.shape[0]
    every_row = lax.all_gather(tokens, "tensor", axis=0, tiled=True)
    gate_up_w = jnp.concatenate(
        [dequant(gate_int_codes, gate_column_scale), dequant(up_int_codes, up_column_scale)], axis=1
    )
    down_w = dequant(down_int_codes, down_column_scale)
    adapter_columns = jnp.transpose(adapter_shrink_weight, (1, 0, 2)).reshape(
        hidden_columns, present_adapters * ADAPTER_RANK
    )
    joint_w = jnp.concatenate([down_w, adapter_columns], axis=1)
    summed = lax.psum_scatter(
        jnp.dot(every_row, gate_up_w, preferred_element_type=jnp.float32).astype(jnp.bfloat16),
        "dp",
        scatter_dimension=0,
        tiled=True,
    ).astype(jnp.float32)
    hidden = jax.nn.silu(summed[:, :hidden_columns]) * summed[:, hidden_columns:]
    rotated = cross_rotate(local_rotate(hidden)).astype(jnp.bfloat16)
    joint = jnp.dot(
        lax.all_gather(rotated, "dp", axis=0, tiled=True),
        joint_w,
        preferred_element_type=jnp.float32,
    )
    base = joint[:, :model_cols]
    shrink_parts = joint[:, model_cols:].reshape(total_rows, present_adapters, ADAPTER_RANK)
    local_ids = row_adapter_index - lax.axis_index("dp") * present_adapters
    owned = (local_ids[:, None] == jnp.arange(present_adapters, dtype=jnp.int32)[None, :]).astype(
        jnp.float32
    )
    partial_shrink = jnp.sum(owned[:, :, None] * shrink_parts, axis=1)
    shrunk_rows = lax.psum(partial_shrink, ("dp", "tensor"))
    reduced_sum = lax.psum_scatter(
        base.astype(jnp.bfloat16), "tensor", scatter_dimension=0, tiled=True
    ).astype(jnp.float32)
    rows_mine = reduced_sum.shape[0]
    first_row = lax.axis_index("tensor") * rows_mine
    owned_shrunk_rows = lax.dynamic_slice_in_dim(shrunk_rows, first_row, rows_mine, 0)
    owned_adapter_index = lax.dynamic_slice_in_dim(row_adapter_index, first_row, rows_mine, 0)
    reduced_sum = reduced_sum + expanded_rows(
        owned_shrunk_rows, owned_adapter_index, adapter_expand_weight
    )
    return reduced_sum.astype(jnp.bfloat16)


def solution(mesh):
    return jax.shard_map(
        body,
        mesh=mesh,
        in_specs=(
            P("tensor", "dp"),
            P("dp", "tensor"),
            P("dp", "tensor"),
            P("tensor", "dp"),
            P("tensor"),
            P("tensor"),
            P("dp"),
            P(),
            P("dp", "tensor", None),
            P(None, None, "dp"),
        ),
        out_specs=P("tensor", "dp"),
        check_vma=False,
    )
```

profile of v0, /device:TPU:1, one launch (start us, length us, event | category | flops | bytes accessed | tf_op | source)
XLA Modules:
  0.0 448.3 jit_solution(17854375020103708834)
XLA Ops:
  6.5 0.7 all-gather.3.cloned.1.call-update
  7.3 0.0 reduce-scatter.7.cloned.1.call-start
  7.3 6.0 %multiply_convert_fusion.1 = (bf16[512,3328]{1,0:T(8,128)(2,1)S(1)}, bf16[512,3328]{1,0:T(8,128)(2,1)}) fusion(bf16[512,3328]{1,0:T(8,128)(2,1)} %param.12, f32[3328]{0:T(1024)} %param.15, f32[3328]{0:T(1024)} %param.14, bf16[512,3328]{1,0:T(8,128)(2,1)} %param.11), kind=kLoop, calls=%fused_computation.6 | loop fusion | flops 10223616 | bytes 13658112 | tf_op jit(solution)/shard_map/convert_element_type | solution.py:34
  13.3 22.8 %all-gather.3.cloned.1.call-done = bf16[1024,512]{1,0:T(8,128)(2,1)} async-done(((bf16[128,512]{1,0:T(8,128)(2,1)}), bf16[1024,512]{1,0:T(8,128)(2,1)}) %all-gather.3.cloned.1.call-update) | async-done | bytes 1048592 | tf_op jit(solution)/shard_map/all_gather | solution.py:96
  36.1 12.7 %convert_bitcast_fusion = bf16[1024,6656]{0,1:T(8,128)(2,1)} fusion(bf16[1024,512]{1,0:T(8,128)(2,1)} %all-gather.3.cloned.1.call-done, bf16[512,3328]{1,0:T(8,128)(2,1)S(1)} %get-tuple-element.7, bf16[512,3328]{1,0:T(8,128)(2,1)} %get-tuple-element.8), kind=kOutput, calls=%fused_computation.1 | convolution fusion | flops 6999769088 | bytes 21495808 | tf_op jit(solution)/shard_map/dot_general | solution.py:106
  48.7 17.4 %copy.29 = bf16[1024,6656]{1,0:T(8,128)(2,1)} copy(bf16[1024,6656]{0,1:T(8,128)(2,1)} %convert_bitcast_fusion) | data formatting | bytes 27262976
  66.1 0.0 reduce-scatter.7.cloned.1.call-update
  66.1 0.2 all-gather.5.cloned.1.call-start
  66.3 97.2 %reduce-scatter.7.cloned.1.call-done = bf16[64,6656]{1,0:T(8,128)(2,1)} async-done(((bf16[1024,6656]{1,0:T(8,128)(2,1)}), bf16[64,6656]{1,0:T(8,128)(2,1)}) %reduce-scatter.7.cloned.1.call-update) | async-done | bytes 851984
  163.5 1.9 copy.30
  165.4 0.2 convert_element_type.88
  165.6 0.4 slice_multiply_fusion
  166.1 2.9 fusion.12
  169.0 1.4 fusion.8
  170.5 0.3 convert_element_type.100
  170.8 0.5 broadcast.64
  171.3 3.2 reduce.2
  174.4 0.2 reshape.78
  174.6 13.3 %all_to_all.36 = bf16[8,2,13312]{2,1,0:T(2,128)(2,1)S(1)} all-to-all(bf16[8,2,13312]{2,1,0:T(2,128)(2,1)S(1)} %reshape.78), channel_id=1, replica_groups=mesh['dp'=16,'tensor'=8] {'tensor'}, dimensions={0} | all-to-all | bytes 851968 | tf_op jit(solution)/shard_map/all_to_all | solution.py:54
  187.9 0.4 reshape.79
  188.4 0.0 copy-start.2
  188.4 0.5 fusion.7
  188.9 0.1 copy.21
  189.0 12.5 %all_to_all.37 = bf16[8,8,3328]{2,0,1:T(8,128)(2,1)} all-to-all(bf16[8,8,3328]{2,0,1:T(8,128)(2,1)S(1)} %copy.21), channel_id=1, replica_groups=mesh['dp'=16,'tensor'=8] {'tensor'}, dimensions={1} | all-to-all | bytes 851968 | tf_op jit(solution)/shard_map/all_to_all | solution.py:64
  201.5 0.0 all-gather.5.cloned.1.call-update
  201.5 0.3 all-reduce.2.cloned.1.call-start
  201.8 3.8 copy.22
  205.6 2.5 multiply_convert_fusion
  208.1 54.3 %all-gather.5.cloned.1.call-done = bf16[1024,3328]{1,0:T(8,128)(2,1)} async-done(((bf16[64,3328]{1,0:T(8,128)(2,1)}), bf16[1024,3328]{1,0:T(8,128)(2,1)}) %all-gather.5.cloned.1.call-update) | async-done | bytes 6815760 | tf_op jit(solution)/shard_map/all_gather | solution.py:114
  262.5 9.2 %fusion.3 = f32[1024,768]{0,1:T(8,128)S(1)} fusion(bf16[1024,3328]{1,0:T(8,128)(2,1)} %all-gather.5.cloned.1.call-done, bf16[3328,256]{1,0:T(8,128)(2,1)} %copy.22, bf16[3328,512]{1,0:T(8,128)(2,1)} %multiply_convert_fusion), kind=kOutput, calls=%fused_computation.8 | convolution fusion | flops 5244715008 | bytes 15073280 | tf_op jit(solution)/shard_map/dot_general | solution.py:113
  271.7 1.6 copy-done.1
  273.4 0.1 slice.22
  273.4 0.7 multiply_reduce_fusion.1
  274.2 0.0 all-reduce.2.cloned.1.call-update
  274.2 0.0 reduce-scatter.9.cloned.1.call-start
  274.2 1.7 slice.26
  276.0 1.3 copy.31
  277.3 0.0 reduce-scatter.9.cloned.1.call-update
  277.3 0.1 compare_and_fusion
  277.4 2.9 gather_fusion
  280.3 131.4 %all-reduce.2.cloned.1.call-done = f32[1024,16]{0,1:T(8,128)} async-done(((f32[1024,16]{0,1:T(8,128)}), f32[1024,16]{0,1:T(8,128)}) %all-reduce.2.cloned.1.call-update) | async-done | bytes 65552 | tf_op jit(solution)/shard_map/psum | solution.py:125
  411.8 0.7 constant_dynamic-slice_fusion
  412.4 0.1 copy.34
  412.6 1.2 multiply_reduce_fusion
  413.8 0.1 copy.28
  413.9 26.0 %reduce-scatter.9.cloned.1.call-done = bf16[128,512]{1,0:T(8,128)(2,1)} async-done(((bf16[1024,512]{1,0:T(8,128)(2,1)}), bf16[128,512]{1,0:T(8,128)(2,1)}) %reduce-scatter.9.cloned.1.call-update) | async-done | bytes 131088
  439.9 1.0 copy.32
  441.0 0.8 copy.23
  (12 shorter events, 0.1 us)
Async XLA Ops:
  6.5 29.5 %all-gather.3.cloned.1.call-start = ((), (), s32[]{:S(2)}) async-start(), calls=%async_computation.4 | async-start | bytes 1179648 | tf_op jit(solution)/shard_map/all_gather | solution.py:96
  7.3 156.3 %reduce-scatter.7.cloned.1.call-start = ((), (), s32[]{:S(2)}) async-start(), calls=%async_computation.7 | async-start | bytes 14483456
  66.1 196.4 %all-gather.5.cloned.1.call-start = ((), (), s32[]{:S(2)}) async-start(), calls=%async_computation.5 | async-start | bytes 7241728 | tf_op jit(solution)/shard_map/all_gather | solution.py:114
  188.4 17.2 %copy-start.2 = (s32[1024]{0:T(1024)S(1)}, s32[1024]{0:T(1024)}, u32[]{:S(2)}) copy-start(s32[1024]{0:T(1024)} %param.17) | copy-start | bytes 12292
  188.4 17.2 %copy-start = (bf16[3328,512]{1,0:T(8,128)(2,1)S(1)}, bf16[3328,512]{1,0:T(8,128)(2,1)}, u32[]{:S(2)}) copy-start(bf16[3328,512]{1,0:T(8,128)(2,1)} %param.13) | copy-start | bytes 10223620
  188.4 17.2 %copy-start.3 = (f32[512]{0:T(512)S(1)}, f32[512]{0:T(512)}, u32[]{:S(2)}) copy-start(f32[512]{0:T(512)} %param.16) | copy-start | bytes 6148
  201.5 210.2 %all-reduce.2.cloned.1.call-start = ((), (), s32[]{:S(2)}) async-start(), calls=%async_computation.6 | async-start | bytes 131072 | tf_op jit(solution)/shard_map/psum | solution.py:125
  271.7 1.6 copy-start.1
  274.2 165.8 %reduce-scatter.9.cloned.1.call-start = ((), (), s32[]{:S(2)}) async-start(), calls=%async_computation.8 | async-start | bytes 1179648
Sparse Core Ops, SparseCore 0:
  9.1 26.9 all-gather.2
  66.2 97.2 reduce-scatter.6
  201.6 60.7 all-gather.4
  274.3 137.3 all-reduce.1
  414.0 25.9 reduce-scatter.8
where the time goes:
time: 451 us; the launch traced here: 448 us
  waiting for transfers between devices  333 us (74%)
  local copies, waits for them, and re-layouts  34.8 us (8%)
  matrix products  26.8 us (6%)
  blocking collectives  25.8 us (6%)
  other arithmetic  14.4 us (3%)
  between operations  13.4 us (3%)
    psum x1, waiting for transfers between devices, body(): shrunk_rows = lax.psum(partial_shrink, ('dp', 'tensor'))  131 us
    unnamed x7, waiting for transfers between devices  124 us
    all_gather x1, waiting for transfers between devices, body(): lax.all_gather(rotated, 'dp', axis=0, tiled=True)  54.3 us
    unnamed x16, local copies, waits for them, and re-layouts  23.9 us
    all_gather x1, waiting for transfers between devices, body(): every_row = lax.all_gather(tokens, 'tensor', axis=0, tiled=True)  22.8 us
    all_to_all x1, blocking collectives, cross_rotate(): lax.all_to_all(values.reshape(rows_here, 1, columns).astype(jnp.bfloat16)...  13.3 us
    dot_general x1, matrix products, body(): jnp.dot(every_row, gate_up_w, preferred_element_type=jnp.float32)  12.7 us
    all_to_all x1, blocking collectives, cross_rotate(): lax.all_to_all(shortened(mixed_vals), 'tensor', split_axis=1, concat_axis...  12.5 us
  transfers between devices with their start and end apart: 5, of which 5 were waited for; matrix products, arithmetic and copies ran while one was open for 5% of the time, Pallas kernels for 0%

commit v1 on v0

v1 whole, which is shorter than its diff:
```python
import math

import jax
import jax.numpy as jnp
import numpy as np
from jax import lax
from jax.experimental import pallas as pl
from jax.experimental.pallas import tpu as pltpu
from jax.sharding import PartitionSpec as P

FACTOR = 13
ADAPTER_RANK = 16
MESH = pl.DeviceIdType.MESH
F32, BF16 = jnp.float32, jnp.bfloat16


def sylvester_signs(order):
    i = np.arange(order)
    common = i[:, None] & i[None, :]
    parity = np.zeros_like(common)
    while common.any():
        parity ^= common & 1
        common = common >> 1
    return 1 - 2 * parity


def hartley_entries(order):
    i = np.arange(order)
    angle = 2.0 * np.pi * ((i[:, None] * i[None, :]) % order) / order
    return (np.cos(angle) + np.sin(angle)) / math.sqrt(order)


def order_of(j):
    return (2 - j + (j // 2) * (7 - 2 * j)) % 4


def first_kernel(
    tok, wg_hbm, wu_hbm, sg, su, signs, out,
    xb, wg, wu, p, r1, r2, t1, t2, hid, mid,
    load_sem, gs, gr, s1s, s1r, s2s, s2r,
):
    dp, tensor = lax.axis_index("dp"), lax.axis_index("tensor")
    z, y = dp // 4, dp % 4
    x, core = tensor // 2, tensor % 2
    cols = wg.shape[1]

    def at_x(step, c):
        return (dp, ((x + step) % 4) * 2 + c)

    def at_z(step):
        return (((z + step) % 4) * 4 + y, tensor)

    def at_y(step):
        return (z * 4 + (y + step) % 4, tensor)

    loads = [
        pltpu.make_async_copy(tok, xb.at[x, pl.ds(2 * core, 2)], load_sem.at[0]),
        pltpu.make_async_copy(wg_hbm, wg, load_sem.at[1]),
        pltpu.make_async_copy(wu_hbm, wu, load_sem.at[2]),
    ]
    for load in loads:
        load.start()

    near = [at_x(0, 1 - core), at_x(1, core), at_x(3, core), at_z(1), at_z(3), at_y(1), at_y(3)]
    barrier = pltpu.get_barrier_semaphore()
    for who in near:
        pl.semaphore_signal(barrier, inc=1, device_id=who, device_id_type=MESH)
    pl.semaphore_wait(barrier, len(near))

    def remote(src, dst, send, recv, who):
        return pltpu.make_async_remote_copy(
            src_ref=src, dst_ref=dst, send_sem=send, recv_sem=recv, device_id=who, device_id_type=MESH
        )

    def shard(step, c):
        return xb.at[(x + step) % 4, pl.ds(2 * c, 2)]

    def part(step, c, h):
        return xb.at[(x + step) % 4, 2 * c + h]

    mate = at_x(0, 1 - core)

    def gather_copy(i, src, dst, who):
        return remote(src, dst, gs.at[i], gr.at[i], who)

    g_sends = [
        gather_copy(0, tok, shard(0, core), mate),
        gather_copy(1, tok, shard(0, core), at_x(1, core)),
        gather_copy(2, tok, shard(0, core), at_x(3, core)),
    ]
    for c in g_sends:
        c.start()

    def landed(i, ref):
        gather_copy(i, ref, ref, mate).wait_recv()

    def pass_on(i, ref, who):
        c = gather_copy(i, ref, ref, who)
        c.start()
        g_sends.append(c)

    landed(1, shard(3, core))
    pass_on(3, part(3, core, 0), at_x(1, core))
    pass_on(5, shard(3, core), mate)
    landed(2, shard(1, core))
    pass_on(4, part(1, core, 1), at_x(3, core))
    pass_on(6, shard(1, core), mate)
    landed(3, part(2, core, 0))
    pass_on(7, part(2, core, 0), mate)
    landed(4, part(2, core, 1))
    pass_on(8, part(2, core, 1), mate)
    for load in loads:
        load.wait()
    landed(0, shard(0, 1 - core))
    landed(5, shard(3, 1 - core))
    landed(6, shard(1, 1 - core))
    landed(7, part(2, 1 - core, 0))
    landed(8, part(2, 1 - core, 1))

    first, second = (z, y), (y, z)
    along = ((at_z, at_y), (at_y, at_z))

    def rows(h):
        return pl.ds(pl.multiple_of(32 * h, 32), 32)

    def stage1(m, s, kind, k):
        step = 1 + 2 * s
        b = (second[m] + order_of(k)) % 4
        a = (first[m] + (2 if kind == 0 else step)) % 4
        h = 1 - s if kind == 1 else s
        src = p.at[m, a, b, rows(h)]
        dst = r1.at[m, s, b] if kind == 0 else r2.at[m, s, b, rows(h)]
        return remote(src, dst, s1s.at[m, s, kind, k], s1r.at[m, s, kind, k], along[m][0](step))

    def stage2(m, s, kind):
        step = 1 + 2 * s
        b = (second[m] + (2 if kind == 0 else step)) % 4
        h = 1 - s if kind == 1 else s
        src = p.at[m, first[m], b, rows(h)]
        dst = t1.at[m, s] if kind == 0 else t2.at[m, s, rows(h)]
        return remote(src, dst, s2s.at[m, s, kind], s2r.at[m, s, kind], along[m][1](step))

    def each(count, do):
        lax.fori_loop(0, count, lambda i, carry: (do(i), carry)[1], 0)

    def chunk(j):
        for m, w in ((0, wg), (1, wu)):
            a = (first[m] + order_of(j)) % 4
            xs = (xb[a] if m == 0 else xb[:, a]).reshape(256, xb.shape[-1])
            for n in range(cols // 256):
                block = slice(n * 256, n * 256 + 256)
                r = jnp.dot(xs, w[:, block], preferred_element_type=F32).astype(BF16)
                p[m, a, :, :, block] = r.reshape(4, 64, 256)

        @pl.when(j == 0)
        def _():
            @pl.loop(0, 4)
            def _(k):
                for m in range(2):
                    for s in range(2):
                        stage1(m, s, 0, k).start()

        @pl.when((j == 1) | (j == 2))
        def _():
            @pl.loop(0, 4)
            def _(k):
                for m in range(2):
                    stage1(m, j - 1, 1, k).start()

    each(4, chunk)

    def add(dst, *refs):
        def group(i):
            r = pl.ds(pl.multiple_of(i * 16, 16), 16)
            v = dst[r, :].astype(F32)
            for ref in refs:
                v = v + ref[r, :].astype(F32)
            dst[r, :] = v.astype(BF16)

        each(dst.shape[0] // 16, group)

    def relay(k):
        for m in range(2):
            for s in range(2):
                stage1(m, s, 0, k).wait_recv()
                b = (second[m] + order_of(k)) % 4
                add(p.at[m, (first[m] + 1 + 2 * s) % 4, b, rows(s)], r1.at[m, s, b])
                stage1(m, s, 2, k).start()

    each(4, relay)

    def settle(m, k):
        b = (second[m] + order_of(k)) % 4
        for s in range(2):
            stage1(m, s, 1, k).wait_recv()
            stage1(m, s, 2, k).wait_recv()
        add(p.at[m, first[m], b], r2.at[m, 0, b], r2.at[m, 1, b])

    for m in range(2):
        settle(m, 0)
        for s in range(2):
            stage2(m, s, 0).start()
    for s in range(2):
        for m in range(2):
            settle(m, 1 + s)
            stage2(m, s, 1).start()
    for s in range(2):
        for m in range(2):
            stage2(m, s, 0).wait_recv()
            add(p.at[m, first[m], (second[m] + 1 + 2 * s) % 4, rows(s)], t1.at[m, s])
            stage2(m, s, 2).start()
    for m in range(2):
        settle(m, 3)
    for m in range(2):
        for s in range(2):
            stage2(m, s, 1).wait_recv()
            stage2(m, s, 2).wait_recv()

    def gated(i):
        r = pl.ds(pl.multiple_of(i * 16, 16), 16)
        g, u = (
            p[m, first[m], second[m], r, :].astype(F32) + t2[m, 0, r, :].astype(F32) + t2[m, 1, r, :].astype(F32)
            for m in range(2)
        )
        g, u = g * sg[...], u * su[...]
        hid[r, :] = g / (1.0 + jnp.exp(-g)) * u

    each(4, gated)
    coef = hartley_entries(FACTOR) / math.sqrt(2048)

    def factor(i):
        r = pl.ds(pl.multiple_of(i * 16, 16), 16)
        blocks = [hid[r, a * 256 : a * 256 + 256] for a in range(FACTOR)]
        for b in range(FACTOR):
            v = blocks[0] * float(coef[b, 0])
            for a in range(1, FACTOR):
                v = v + blocks[a] * float(coef[b, a])
            mid[b, r, :] = v.astype(BF16)

    each(4, factor)
    for b in range(FACTOR):
        out[:, b * 256 : b * 256 + 256] = jnp.dot(mid[b], signs[...], preferred_element_type=F32).astype(BF16)

    for c in g_sends:
        c.wait_send()

    @pl.loop(0, 4)
    def _(k):
        for m in range(2):
            for s in range(2):
                for kind in range(3):
                    stage1(m, s, kind, k).wait_send()

    for m in range(2):
        for s in range(2):
            for kind in range(3):
                stage2(m, s, kind).wait_send()


def gate_up(tokens, gate_codes, up_codes, gate_scale, up_scale):
    width, cols = gate_codes.shape
    vmem = pl.BlockSpec(memory_space=pltpu.VMEM)
    hbm = pl.BlockSpec(memory_space=pl.ANY)
    dma = pltpu.SemaphoreType.DMA
    return pl.pallas_call(
        first_kernel,
        out_shape=jax.ShapeDtypeStruct((64, cols), BF16),
        in_specs=[hbm, hbm, hbm, vmem, vmem, vmem],
        out_specs=vmem,
        scratch_shapes=[
            pltpu.VMEM((4, 4, 64, width), BF16),
            pltpu.VMEM((width, cols), BF16),
            pltpu.VMEM((width, cols), BF16),
            pltpu.VMEM((2, 4, 4, 64, cols), BF16),
            pltpu.VMEM((2, 2, 4, 32, cols), BF16),
            pltpu.VMEM((2, 2, 4, 64, cols), BF16),
            pltpu.VMEM((2, 2, 32, cols), BF16),
            pltpu.VMEM((2, 2, 64, cols), BF16),
            pltpu.VMEM((64, cols), F32),
            pltpu.VMEM((FACTOR, 64, 256), BF16),
            dma((3,)), dma((9,)), dma((9,)),
            dma((2, 2, 3, 4)), dma((2, 2, 3, 4)), dma((2, 2, 3)), dma((2, 2, 3)),
        ],
        compiler_params=pltpu.CompilerParams(
            collective_id=0, has_side_effects=True, vmem_limit_bytes=60 * 1024 * 1024
        ),
        name="gate_up_sum",
    )(
        tokens.reshape(2, 64, width), gate_codes, up_codes,
        gate_scale.reshape(1, cols), up_scale.reshape(1, cols), jnp.asarray(sylvester_signs(256), BF16),
    )


def dequant(codes, scale):
    return (codes.astype(jnp.float32) * scale).astype(jnp.bfloat16)


def cross_rotate(values):
    n_tensor = lax.axis_size("tensor")
    rows_here, columns = values.shape
    signs = jnp.asarray(sylvester_signs(n_tensor), F32)
    mixed_vals = jnp.einsum(
        "rtc,st->rsc",
        lax.all_to_all(
            values.reshape(rows_here, 1, columns), "tensor", split_axis=0, concat_axis=1, tiled=True,
        ).astype(jnp.float32),
        signs,
        precision=lax.Precision.HIGHEST,
    )
    outcome = lax.all_to_all(mixed_vals.astype(BF16), "tensor", split_axis=1, concat_axis=0, tiled=True)
    return outcome.reshape(rows_here, columns)


def expanded_rows(shrunk_rows, selected_adapter_index, adapter_expand_weight):
    selected_rows = jnp.take(adapter_expand_weight, selected_adapter_index, axis=0)
    return jnp.einsum(
        "rk,rkd->rd", shrunk_rows, selected_rows.astype(jnp.float32), precision=lax.Precision.HIGHEST,
    )


def body(
    tokens, gate_int_codes, up_int_codes, down_int_codes, gate_column_scale, up_column_scale, down_column_scale,
    row_adapter_index, adapter_shrink_weight, adapter_expand_weight,
):
    total_rows = row_adapter_index.shape[0]
    hidden_columns = gate_int_codes.shape[1]
    model_cols = down_int_codes.shape[1]
    present_adapters = adapter_shrink_weight.shape[0]
    down_w = dequant(down_int_codes, down_column_scale)
    adapter_columns = jnp.transpose(adapter_shrink_weight, (1, 0, 2)).reshape(
        hidden_columns, present_adapters * ADAPTER_RANK
    )
    joint_w = jnp.concatenate([down_w, adapter_columns], axis=1)
    local = gate_up(tokens, gate_int_codes, up_int_codes, gate_column_scale, up_column_scale)
    rotated = cross_rotate(local)
    joint = jnp.dot(
        lax.all_gather(rotated, "dp", axis=0, tiled=True), joint_w, preferred_element_type=jnp.float32,
    )
    base = joint[:, :model_cols]
    shrink_parts = joint[:, model_cols:].reshape(total_rows, present_adapters, ADAPTER_RANK)
    local_ids = row_adapter_index - lax.axis_index("dp") * present_adapters
    owned = (local_ids[:, None] == jnp.arange(present_adapters, dtype=jnp.int32)[None, :]).astype(jnp.float32)
    partial_shrink = jnp.sum(owned[:, :, None] * shrink_parts, axis=1)
    shrunk_rows = lax.psum(partial_shrink, ("dp", "tensor"))
    reduced_sum = lax.psum_scatter(
        base.astype(jnp.bfloat16), "tensor", scatter_dimension=0, tiled=True
    ).astype(jnp.float32)
    rows_mine = reduced_sum.shape[0]
    first_row = lax.axis_index("tensor") * rows_mine
    owned_shrunk_rows = lax.dynamic_slice_in_dim(shrunk_rows, first_row, rows_mine, 0)
    owned_adapter_index = lax.dynamic_slice_in_dim(row_adapter_index, first_row, rows_mine, 0)
    reduced_sum = reduced_sum + expanded_rows(owned_shrunk_rows, owned_adapter_index, adapter_expand_weight)
    return reduced_sum.astype(jnp.bfloat16)


def solution(mesh):
    return jax.shard_map(
        body,
        mesh=mesh,
        in_specs=(
            P("tensor", "dp"), P("dp", "tensor"), P("dp", "tensor"), P("tensor", "dp"), P("tensor"), P("tensor"),
            P("dp"), P(), P("dp", "tensor", None), P(None, None, "dp"),
        ),
        out_specs=P("tensor", "dp"),
        check_vma=False,
    )
```

time: 451 us -> 381 us (0.84)
  waiting for transfers between devices: 333 us -> 212 us
  Pallas kernels: 0 us -> 93.9 us
  matrix products: 26.8 us -> 9.72 us
  local copies, waits for them, and re-layouts: 34.8 us -> 18 us
  other arithmetic: 14.4 us -> 6.49 us
    unnamed x7 -> x4, waiting for transfers between devices: 124 us -> 26.4 us
    pallas_call x0 -> x1, Pallas kernels: none -> 93.9 us  [gate_up(): pl.pallas_call(first_kernel, out_shape=jax.ShapeDtypeStruct((64, cols), B...]
    all_gather x1 -> x0, waiting for transfers between devices: 22.8 us -> none  [body(): every_row = lax.all_gather(tokens, 'tensor', axis=0, tiled=True)]
    unnamed x16, local copies, waits for them, and re-layouts: 23.9 us -> 4.72 us
    dot_general x3 -> x0, matrix products: 17 us -> none  [the longest x1 12.7 us: body(): jnp.dot(every_row, gate_up_w, preferred_element_type=jnp.float32)]
    convert_element_type x2 -> x1, other arithmetic: 8.5 us -> 2.52 us  [dequant(): return (codes.astype(jnp.float32) * scale).astype(jnp.bfloat16)]
  transfers between devices with their start and end apart: 5 -> 3, of which waited for: 5 -> 3; matrix products, arithmetic and copies ran while one was open for 5% -> 4% of each run, Pallas kernels for 0% -> 0%
where the time goes in v1:
time: 381 us; the launch traced here: 378 us
  waiting for transfers between devices  212 us (56%)
  Pallas kernels  93.9 us (25%)
  blocking collectives  24.6 us (6%)
  local copies, waits for them, and re-layouts  18 us (5%)
  between operations  13.3 us (3%)
  matrix products  9.72 us (3%)
  other arithmetic  6.49 us (2%)
    psum x1, waiting for transfers between devices, body(): shrunk_rows = lax.psum(partial_shrink, ('dp', 'tensor'))  131 us
    pallas_call x1, Pallas kernels, gate_up(): pl.pallas_call(first_kernel, out_shape=jax.ShapeDtypeStruct((64, cols), B...  93.9 us
    all_gather x1, waiting for transfers between devices, body(): lax.all_gather(rotated, 'dp', axis=0, tiled=True)  54.4 us
    unnamed x4, waiting for transfers between devices  26.4 us
    all_to_all x1, blocking collectives, cross_rotate(): lax.all_to_all(mixed_vals.astype(BF16), 'tensor', split_axis=1, concat_ax...  12.5 us
    all_to_all x1, blocking collectives, cross_rotate(): lax.all_to_all(values.reshape(rows_here, 1, columns), 'tensor', split_axi...  12.1 us
    dot_general x1, matrix products, body(): jnp.dot(lax.all_gather(rotated, 'dp', axis=0, tiled=True), joint_w, prefe...  9.24 us
  transfers between devices with their start and end apart: 3, of which 3 were waited for; matrix products, arithmetic and copies ran while one was open for 4% of the time, Pallas kernels for 0%

profile of v1, /device:TPU:1, one launch (start us, length us, event | category | flops | bytes accessed | tf_op | source)
XLA Modules:
  0.0 378.3 jit_solution(16255830830394262004)
XLA Ops:
  6.5 0.0 all-gather.2.cloned.1.call-start
  6.5 1.3 reshape.51.sg
  7.9 1.3 reshape.52.su
  9.2 93.9 %gate_up_sum.1 = bf16[64,3328]{1,0:T(8,128)(2,1)} custom-call(bf16[2,64,512]{2,1,0:T(8,128)(2,1)} %bitcast.30, bf16[512,3328]{1,0:T(8,128)(2,1)} %wg_hbm.1, bf16[512,3328]{1,0:T(8,128)(2,1)} %wu_hbm.1, f32[1,3328]{1,0:T(1,128)} %reshape.51.sg, f32[1,3328]{1,0:T(1,128)} %reshape.52.su, bf16[256,256]{1,0:T(8,128)(2,1)} %constant.38.clone.signs), custom_call_target="tpu_custom_call" | custom-call | tf_op jit(solution)/shard_map/gate_up_sum/pallas_call | solution.py:265
  103.1 0.0 copy-start.3
  103.1 0.5 broadcast.23
  103.7 1.9 reduce.2
  105.6 0.2 reshape.71
  105.7 12.1 %all_to_all.33 = bf16[8,2,13312]{2,1,0:T(2,128)(2,1)S(1)} all-to-all(bf16[8,2,13312]{2,1,0:T(2,128)(2,1)S(1)} %reshape.71), channel_id=1, replica_groups=mesh['dp'=16,'tensor'=8] {'tensor'}, dimensions={0} | all-to-all | bytes 851968 | tf_op jit(solution)/shard_map/all_to_all | solution.py:304
  117.8 0.4 reshape.72
  118.2 0.0 copy-start.2
  118.2 0.0 copy-start
  118.2 0.0 copy-start.4
  118.3 0.0 copy-done.3
  118.3 0.5 fusion.4
  118.8 0.1 copy.26
  118.8 12.5 %all_to_all.34 = bf16[8,8,3328]{2,0,1:T(8,128)(2,1)} all-to-all(bf16[8,8,3328]{2,0,1:T(8,128)(2,1)S(1)} %copy.26), channel_id=1, replica_groups=mesh['dp'=16,'tensor'=8] {'tensor'}, dimensions={1} | all-to-all | bytes 851968 | tf_op jit(solution)/shard_map/all_to_all | solution.py:310
  131.4 0.0 all-gather.2.cloned.1.call-update
  131.4 0.0 all-reduce.2.cloned.1.call-start
  131.4 3.8 copy.27
  135.2 0.0 copy-done.2
  135.2 0.0 copy-done
  135.2 0.0 copy-done.4
  135.3 2.5 multiply_convert_fusion
  137.8 54.4 %all-gather.2.cloned.1.call-done = bf16[1024,3328]{1,0:T(8,128)(2,1)} async-done(((bf16[64,3328]{1,0:T(8,128)(2,1)}), bf16[1024,3328]{1,0:T(8,128)(2,1)}) %all-gather.2.cloned.1.call-update) | async-done | bytes 6815760 | tf_op jit(solution)/shard_map/all_gather | solution.py:337
  192.2 9.2 %fusion = f32[1024,768]{0,1:T(8,128)S(1)} fusion(bf16[1024,3328]{1,0:T(8,128)(2,1)} %all-gather.2.cloned.1.call-done, bf16[3328,256]{1,0:T(8,128)(2,1)} %copy.27, bf16[3328,512]{1,0:T(8,128)(2,1)} %multiply_convert_fusion), kind=kOutput, calls=%fused_computation.2 | convolution fusion | flops 5244715008 | bytes 15073280 | tf_op jit(solution)/shard_map/dot_general | solution.py:336
  201.4 0.0 copy-start.1
  201.4 1.7 copy-done.1
  203.1 0.1 slice.12
  203.2 0.7 multiply_reduce_fusion.1
  203.9 0.0 all-reduce.2.cloned.1.call-update
  203.9 0.0 reduce-scatter.4.cloned.1.call-start
  204.0 1.7 slice.14
  205.7 1.3 copy.33
  207.1 0.0 reduce-scatter.4.cloned.1.call-update
  207.1 0.1 compare_and_fusion
  207.2 2.9 gather_fusion
  210.1 131.4 %all-reduce.2.cloned.1.call-done = f32[1024,16]{0,1:T(8,128)} async-done(((f32[1024,16]{0,1:T(8,128)}), f32[1024,16]{0,1:T(8,128)}) %all-reduce.2.cloned.1.call-update) | async-done | bytes 65552 | tf_op jit(solution)/shard_map/psum | solution.py:344
  341.4 0.7 constant_dynamic-slice_fusion
  342.2 0.1 copy.36
  342.3 1.2 multiply_reduce_fusion
  343.5 0.1 copy.32
  343.6 26.3 %reduce-scatter.4.cloned.1.call-done = bf16[128,512]{1,0:T(8,128)(2,1)} async-done(((bf16[1024,512]{1,0:T(8,128)(2,1)}), bf16[128,512]{1,0:T(8,128)(2,1)}) %reduce-scatter.4.cloned.1.call-update) | async-done | bytes 131088
  369.9 1.0 copy.34
  371.0 0.8 copy.28
  (5 shorter events, 0.1 us)
Async XLA Ops:
  6.5 185.7 %all-gather.2.cloned.1.call-start = ((), (), s32[]{:S(2)}) async-start(), calls=%async_computation.3 | async-start | bytes 7241728 | tf_op jit(solution)/shard_map/all_gather | solution.py:337
  103.1 15.1 %copy-start.3 = (f32[8,8,1]{1,0,2:T(8,128)S(1)}, f32[8,8,1]{1,0,2:T(8,128)}, u32[]{:S(2)}) copy-start(f32[8,8,1]{1,0,2:T(8,128)} %constant.41) | copy-start | bytes 772
  118.2 17.0 %copy-start.2 = (s32[1024]{0:T(1024)S(1)}, s32[1024]{0:T(1024)}, u32[]{:S(2)}) copy-start(s32[1024]{0:T(1024)} %param.19) | copy-start | bytes 12292
  118.2 17.0 %copy-start = (bf16[3328,512]{1,0:T(8,128)(2,1)S(1)}, bf16[3328,512]{1,0:T(8,128)(2,1)}, u32[]{:S(2)}) copy-start(bf16[3328,512]{1,0:T(8,128)(2,1)} %param.15) | copy-start | bytes 10223620
  118.2 17.0 %copy-start.4 = (f32[512]{0:T(512)S(1)}, f32[512]{0:T(512)}, u32[]{:S(2)}) copy-start(f32[512]{0:T(512)} %param.18) | copy-start | bytes 6148
  131.4 210.1 %all-reduce.2.cloned.1.call-start = ((), (), s32[]{:S(2)}) async-start(), calls=%async_computation.4 | async-start | bytes 131072 | tf_op jit(solution)/shard_map/psum | solution.py:344
  201.4 1.7 copy-start.1
  203.9 166.0 %reduce-scatter.4.cloned.1.call-start = ((), (), s32[]{:S(2)}) async-start(), calls=%async_computation.5 | async-start | bytes 1179648
Sparse Core Ops, SparseCore 0:
  131.5 60.6 all-gather.1
  204.1 137.3 all-reduce.1
  344.0 25.9 reduce-scatter.3

commit v2 on v1

v2 whole, which is shorter than its diff:
```python
import math

import jax
import jax.numpy as jnp
import numpy as np
from jax import lax
from jax.experimental import pallas as pl
from jax.experimental.pallas import tpu as pltpu
from jax.sharding import PartitionSpec as P

FACTOR = 13
ADAPTER_RANK = 16
MESH = pl.DeviceIdType.MESH
F32, BF16 = jnp.float32, jnp.bfloat16


def sylvester_signs(order):
    i = np.arange(order)
    common = i[:, None] & i[None, :]
    parity = np.zeros_like(common)
    while common.any():
        parity ^= common & 1
        common = common >> 1
    return 1 - 2 * parity


def hartley_entries(order):
    i = np.arange(order)
    angle = 2.0 * np.pi * ((i[:, None] * i[None, :]) % order) / order
    return (np.cos(angle) + np.sin(angle)) / math.sqrt(order)


def order_of(j):
    return (2 - j + (j // 2) * (7 - 2 * j)) % 4


BATCHES = 2
BATCH_ROWS = 64 // BATCHES
HALF_ROWS = BATCH_ROWS // 2
PART_SPLIT = 8 // (BATCH_ROWS // 16)
PART_COLS = {2: 1664, 4: 896}[PART_SPLIT]


def part_place(t):
    j = t % PART_SPLIT
    first = 1664 * j if PART_SPLIT == 2 else 128 * (6 * j + (j + 2) // 3)
    return t // PART_SPLIT, first


def each(count, do):
    lax.fori_loop(0, count, lambda i, carry: (do(i), carry)[1], 0)


def layer_kernel(
    tok, wg_hbm, wu_hbm, wd_hbm, shrink_hbm, expand_hbm, sg, su, sd, ids, out,
    xb, wg, wu, p, r1, r2, t1, t2, hid, mid, loc, am, bm, cm, rot, wd, ws, we, bs, bsr, sp, spr, spz, spy,
    load_sem, gs, gr, s1s, s1r, s2s, s2r, a_s, a_r, c_s, c_r, g1s, g1r, g2s, g2r, b_s, b_r, h_s, h_r, d_s, d_r,
):
    dp, tensor = lax.axis_index("dp"), lax.axis_index("tensor")
    z, y = dp // 4, dp % 4
    x, core = tensor // 2, tensor % 2
    cols = wg.shape[1]

    def at_x(step, c):
        return (dp, ((x + step) % 4) * 2 + c)

    def at_z(step):
        return (((z + step) % 4) * 4 + y, tensor)

    def at_y(step):
        return (z * 4 + (y + step) % 4, tensor)

    def peer(i):
        return ((x + i // 2) % 4) * 2 + (core + i % 2) % 2

    def before(i):
        return ((x + 4 - i // 2) % 4) * 2 + (core + i % 2) % 2

    far_first = (4, 5, 2, 3, 6, 7, 1)

    loads = [
        pltpu.make_async_copy(tok.at[q, h], xb.at[x, 2 * core + h, pl.ds(32 * q, 32)], load_sem.at[2 * q + h])
        for q in range(2)
        for h in range(2)
    ]
    loads += [
        pltpu.make_async_copy(a, b, load_sem.at[4 + i])
        for i, (a, b) in enumerate(((wg_hbm, wg), (wu_hbm, wu), (wd_hbm, wd), (shrink_hbm, ws), (expand_hbm, we)))
    ]
    for load in loads[:6]:
        load.start()

    near = [at_x(i // 2, (core + i % 2) % 2) for i in range(1, 8)]
    near += [at_z(i) for i in (1, 2, 3)] + [at_y(i) for i in (1, 2, 3)]
    barrier = pltpu.get_barrier_semaphore()
    for who in near:
        pl.semaphore_signal(barrier, inc=1, device_id=who, device_id_type=MESH)
    pl.semaphore_wait(barrier, len(near))

    def remote(src, dst, send, recv, who):
        return pltpu.make_async_remote_copy(
            src_ref=src, dst_ref=dst, send_sem=send, recv_sem=recv, device_id=who, device_id_type=MESH
        )

    def shard(step, c):
        return xb.at[(x + step) % 4, pl.ds(2 * c, 2)]

    def part(step, c, h):
        return xb.at[(x + step) % 4, 2 * c + h]

    mate = at_x(0, 1 - core)
    sent = []

    def launch(copy):
        copy.start()
        sent.append(copy)

    def gather_copy(i, ref, who):
        return remote(ref, ref, gs.at[i], gr.at[i], who)

    def landed(i, ref):
        gather_copy(i, ref, mate).wait_recv()

    def pass_on(i, ref, who):
        launch(gather_copy(i, ref, who))

    for load in loads[:4]:
        load.wait()
    pass_on(1, shard(0, core), at_x(1, core))
    pass_on(2, shard(0, core), at_x(3, core))
    pass_on(0, shard(0, core), mate)
    landed(1, shard(3, core))
    pass_on(3, part(3, core, 0), at_x(1, core))
    pass_on(5, shard(3, core), mate)
    landed(2, shard(1, core))
    pass_on(4, part(1, core, 1), at_x(3, core))
    pass_on(6, shard(1, core), mate)
    landed(3, part(2, core, 0))
    pass_on(7, part(2, core, 0), mate)
    landed(4, part(2, core, 1))
    pass_on(8, part(2, core, 1), mate)
    for load in loads[4:6]:
        load.wait()
    landed(0, shard(0, 1 - core))
    landed(5, shard(3, 1 - core))
    landed(6, shard(1, 1 - core))
    landed(7, part(2, 1 - core, 0))
    landed(8, part(2, 1 - core, 1))

    first, second = (z, y), (y, z)
    along = ((at_z, at_y), (at_y, at_z))

    def rows(q, h):
        return pl.ds(pl.multiple_of(BATCH_ROWS * q + HALF_ROWS * h, HALF_ROWS), HALF_ROWS)

    def batch_rows(q):
        return pl.ds(BATCH_ROWS * q, BATCH_ROWS)

    def half_rows(q):
        return pl.ds(HALF_ROWS * q, HALF_ROWS)

    def stage1(q, m, s, kind, k):
        step = 1 + 2 * s
        b = (second[m] + order_of(k)) % 4
        a = (first[m] + (2 if kind == 0 else step)) % 4
        h = 1 - s if kind == 1 else s
        src = p.at[m, a, b, rows(q, h)]
        dst = r1.at[m, s, b, half_rows(q)] if kind == 0 else r2.at[m, s, b, rows(q, h)]
        i = (q, m, s, kind, k)
        return remote(src, dst, s1s.at[i], s1r.at[i], along[m][0](step))

    def stage2(q, m, s, kind):
        step = 1 + 2 * s
        b = (second[m] + (2 if kind == 0 else step)) % 4
        h = 1 - s if kind == 1 else s
        src = p.at[m, first[m], b, rows(q, h)]
        dst = t1.at[m, s, half_rows(q)] if kind == 0 else t2.at[m, s, rows(q, h)]
        i = (q, m, s, kind)
        return remote(src, dst, s2s.at[i], s2r.at[i], along[m][1](step))

    def send_far(q):
        @pl.loop(0, 4)
        def _(k):
            for m in range(2):
                for s in range(2):
                    stage1(q, m, s, 0, k).start()

    def send_near(q, s):
        @pl.loop(0, 4)
        def _(k):
            for m in range(2):
                stage1(q, m, s, 1, k).start()

    def chunk(j):
        for m, w in ((0, wg), (1, wu)):
            a = (first[m] + order_of(j)) % 4
            xs = (xb[a] if m == 0 else xb[:, a]).reshape(256, xb.shape[-1])
            for n in range(cols // 256):
                block = slice(n * 256, n * 256 + 256)
                r = jnp.dot(xs, w[:, block], preferred_element_type=F32).astype(BF16)
                p[m, a, :, :, block] = r.reshape(4, 64, 256)

        @pl.when(j == 0)
        def _():
            send_far(0)

        @pl.when((j == 1) | (j == 2))
        def _():
            send_near(0, j - 1)

    def add(dst, *refs):
        def group(i):
            r = pl.ds(pl.multiple_of(i * 16, 16), 16)
            v = dst[r, :].astype(F32)
            for ref in refs:
                v = v + ref[r, :].astype(F32)
            dst[r, :] = v.astype(BF16)

        each(dst.shape[0] // 16, group)

    def relay(q):
        def one(k):
            for m in range(2):
                for s in range(2):
                    stage1(q, m, s, 0, k).wait_recv()
                    b = (second[m] + order_of(k)) % 4
                    add(p.at[m, (first[m] + 1 + 2 * s) % 4, b, rows(q, s)], r1.at[m, s, b, half_rows(q)])
                    stage1(q, m, s, 2, k).start()

        each(4, one)

    def settle(q, m, k):
        b = (second[m] + order_of(k)) % 4
        for s in range(2):
            stage1(q, m, s, 1, k).wait_recv()
            stage1(q, m, s, 2, k).wait_recv()
        r = batch_rows(q)
        add(p.at[m, first[m], b, r], r2.at[m, 0, b, r], r2.at[m, 1, b, r])

    def cross_far(q):
        for m in range(2):
            settle(q, m, 0)
            for s in range(2):
                stage2(q, m, s, 0).start()

    def cross_near(q):
        for s in range(2):
            for m in range(2):
                settle(q, m, 1 + s)
                stage2(q, m, s, 1).start()

    def cross_relay(q):
        for s in range(2):
            for m in range(2):
                stage2(q, m, s, 0).wait_recv()
                b = (second[m] + 1 + 2 * s) % 4
                add(p.at[m, first[m], b, rows(q, s)], t1.at[m, s, half_rows(q)])
                stage2(q, m, s, 2).start()

    def cross_end(q):
        for m in range(2):
            settle(q, m, 3)
        for m in range(2):
            for s in range(2):
                stage2(q, m, s, 1).wait_recv()
                stage2(q, m, s, 2).wait_recv()

    coef = hartley_entries(FACTOR) / math.sqrt(2048)
    lanes = lax.broadcasted_iota(jnp.int32, (256, 256), 0) & lax.broadcasted_iota(jnp.int32, (256, 256), 1)
    for shift in (4, 2, 1):
        lanes = lanes ^ (lanes >> shift)
    signs = (1 - 2 * (lanes & 1)).astype(F32).astype(BF16)

    def local_part(q):
        def gated(i):
            r = pl.ds(pl.multiple_of(BATCH_ROWS * q + i * 16, 16), 16)
            g, u = (
                p[m, first[m], second[m], r, :].astype(F32) + t2[m, 0, r, :].astype(F32) + t2[m, 1, r, :].astype(F32)
                for m in range(2)
            )
            g, u = g * sg[...], u * su[...]
            hid[r, :] = g / (1.0 + jnp.exp(-g)) * u

        each(BATCH_ROWS // 16, gated)

        def factor(i):
            r = pl.ds(pl.multiple_of(BATCH_ROWS * q + i * 16, 16), 16)
            blocks = [hid[r, a * 256 : a * 256 + 256] for a in range(FACTOR)]
            for b in range(FACTOR):
                v = blocks[0] * float(coef[b, 0])
                for a in range(1, FACTOR):
                    v = v + blocks[a] * float(coef[b, a])
                mid[b, r, :] = v.astype(BF16)

        each(BATCH_ROWS // 16, factor)
        r = batch_rows(q)
        turned = jnp.dot(
            mid[:, r, :].reshape(FACTOR * BATCH_ROWS, 256), signs, preferred_element_type=F32
        ).astype(BF16)
        for b in range(FACTOR):
            loc[r, b * 256 : b * 256 + 256] = turned[b * BATCH_ROWS : (b + 1) * BATCH_ROWS]
        for i in far_first:
            launch(mix_copy(q, i))
        am[q, tensor] = my_part(q, tensor)[...]

    def my_part(q, t):
        group, start = part_place(t)
        r = pl.ds(pl.multiple_of(BATCH_ROWS * q + 16 * group, 16), 16)
        return loc.at[r, pl.ds(pl.multiple_of(start, 128), PART_COLS)]

    def mix_copy(q, i):
        to = peer(i)
        return remote(my_part(q, to), am.at[q, tensor], a_s.at[q, i], a_r.at[q, i], (dp, to))

    def back_copy(q, i):
        to = peer(i)
        return remote(bm.at[q, to], cm.at[q, tensor], c_s.at[q, i], c_r.at[q, i], (dp, to))

    def mix(q):
        for i in far_first:
            mix_copy(q, i).wait_recv()
        for c in range(PART_COLS // 128):
            lane = slice(c * 128, c * 128 + 128)
            v = [am[q, t, :, lane].astype(F32) for t in range(8)]
            for bit in (1, 2, 4):
                v = [v[t] + v[t ^ bit] if t & bit == 0 else v[t ^ bit] - v[t] for t in range(8)]
            for t in range(8):
                bm[q, t, :, lane] = v[t].astype(BF16)
        for i in far_first:
            launch(back_copy(q, i))
        cm[q, tensor] = bm[q, tensor]

    def off(c):
        return c + (c // 2) * (5 - 2 * c)

    def held(q, f, c1, c2):
        c = (c1 % 4, c2 % 4) if f == 0 else (c2 % 4, c1 % 4)
        return rot.at[c[0], c[1], rows(q, f)]

    def half_cols(s):
        return pl.ds(s * (cols // 2), cols // 2)

    def spread1(q, f, s, kind):
        step = 1 + 2 * s
        ref = held(q, f, first[f] + (0 if kind == 0 else 4 - step), second[f])
        if kind == 1:
            ref = ref.at[:, half_cols(s)]
        i = (q, f, s, kind)
        return remote(ref, ref, g1s.at[i], g1r.at[i], along[f][0](step))

    def spread2(q, f, s, kind, c):
        step = 1 + 2 * s
        ref = held(q, f, first[f] + off(c), second[f] + (0 if kind == 0 else 4 - step))
        if kind == 1:
            ref = ref.at[:, half_cols(s)]
        i = (q, f, s, kind, c)
        return remote(ref, ref, g2s.at[i], g2r.at[i], along[f][1](step))

    def got1(q, f, s, kind):
        step = 1 + 2 * s
        ref = held(q, f, first[f] + (4 - step if kind == 0 else 2), second[f])
        if kind == 1:
            ref = ref.at[:, half_cols(s)]
        i = (q, f, s, kind)
        remote(ref, ref, g1s.at[i], g1r.at[i], along[f][0](step)).wait_recv()

    def got2(q, f, s, kind, c):
        step = 1 + 2 * s
        ref = held(q, f, first[f] + off(c), second[f] + (4 - step if kind == 0 else 2))
        if kind == 1:
            ref = ref.at[:, half_cols(s)]
        i = (q, f, s, kind, c)
        remote(ref, ref, g2s.at[i], g2r.at[i], along[f][1](step)).wait_recv()

    def spread_start(q):
        for i in far_first:
            back_copy(q, i).wait_recv()
        for t in range(8):
            group, start = part_place(t)
            r = pl.ds(BATCH_ROWS * q + 16 * group, 16)
            rot[z, y, r, start : start + PART_COLS] = cm[q, t]
        for f in range(2):
            for s in range(2):
                launch(spread1(q, f, s, 0))
        for f in range(2):
            for s in range(2):
                launch(spread2(q, f, s, 0, 0))

    def spread_mid(q):
        for s in range(2):
            for f in range(2):
                got1(q, f, s, 0)
                launch(spread1(q, f, s, 1))
        for s in range(2):
            for f in range(2):
                for s2 in range(2):
                    launch(spread2(q, f, s2, 0, 2 - s))

    def spread_far(q):
        for f in range(2):
            for s in range(2):
                got1(q, f, s, 1)
            for s2 in range(2):
                launch(spread2(q, f, s2, 0, 3))

    def spread_relay(q, c):
        for f in range(2):
            for s in range(2):
                got2(q, f, s, 0, c)
                launch(spread2(q, f, s, 1, c))

    def spread_end(q):
        for c in range(4):
            for f in range(2):
                for s in range(2):
                    got2(q, f, s, 1, c)

    def sum_copy(q, i):
        to = peer(i)
        return remote(bs.at[q, to], bsr.at[q, tensor], b_s.at[q, i], b_r.at[q, i], (dp, to))

    def down(q):
        def group(g):
            lhs = rot[pl.ds(2 * g, 2), :, batch_rows(q), :].reshape(8 * BATCH_ROWS, cols)
            base = jnp.dot(lhs, wd[...], preferred_element_type=F32).astype(BF16)
            bs[q, pl.ds(4 * g, 4)] = base.reshape(4, 2 * BATCH_ROWS, base.shape[-1])
            parts = lax.dot_general(ws[...], lhs, (((1,), (1,)), ((), ())), preferred_element_type=F32)
            id_row = ids[q, g]
            total = jnp.zeros((ADAPTER_RANK, 8 * BATCH_ROWS), F32)
            for a in range(16):
                mine = id_row == dp * 16 + a
                total = total + jnp.where(mine, parts[a * 16 : a * 16 + 16], 0.0)
            lane = lax.broadcasted_iota(jnp.int32, (ADAPTER_RANK, 128), 1)
            for i in range(2):
                v = total[:, i * 128 : i * 128 + 128]
                turned = pltpu.roll(v, 64, 1)
                even, odd = 4 * g + 2 * i, 4 * g + 2 * i + 1
                if q == 0:
                    sp[even] = v
                    sp[odd] = turned
                else:
                    sp[even] = jnp.where(lane < 64, sp[even], turned)
                    sp[odd] = jnp.where(lane < 64, sp[odd], v)

        each(2, group)
        for i in far_first:
            launch(sum_copy(q, i))

    def shrink_copy(i):
        to = peer(i)
        return remote(sp.at[to], spr.at[tensor], h_s.at[i], h_r.at[i], (dp, to))

    def shrink_z(i):
        return remote(spz.at[z], spz.at[z], d_s.at[0, i], d_r.at[0, i], at_z(i))

    def shrink_y(i):
        return remote(spy.at[y], spy.at[y], d_s.at[1, i], d_r.at[1, i], at_y(i))

    def total(refs):
        v = refs[0]
        for ref in refs[1:]:
            v = v + ref
        return v

    def finish():
        for i in far_first:
            launch(shrink_copy(i))
        for i in far_first:
            shrink_copy(i).wait_recv()
        spr[tensor] = sp[tensor]
        spz[z] = total([spr[t] for t in range(8)])
        for i in (2, 1, 3):
            launch(shrink_z(i))
        for i in (2, 1, 3):
            shrink_z(i).wait_recv()
        spy[y] = total([spz[c] for c in range(4)])
        for i in (2, 1, 3):
            launch(shrink_y(i))
        for q in range(BATCHES):
            for i in far_first:
                sum_copy(q, i).wait_recv()
            bsr[q, tensor] = bs[q, tensor]
        for i in (2, 1, 3):
            shrink_y(i).wait_recv()
        shrunk = total([spy[c] for c in range(4)])
        wide = jnp.concatenate([shrunk] * 8, axis=0).T
        own_ids = jnp.broadcast_to(ids[2, tensor, :, :128], (128, 128)).astype(F32).T
        lane_adapter = (lax.broadcasted_iota(jnp.int32, (128, 128), 1) // ADAPTER_RANK).astype(F32)
        spot = own_ids - lane_adapter
        chosen = jnp.concatenate(
            [jnp.where(spot == float(8 * j), wide, 0.0).astype(BF16) for j in range(32)], axis=1
        )
        extra = jnp.dot(chosen, we[...], preferred_element_type=F32)
        for q in range(BATCHES):
            r = slice(2 * BATCH_ROWS * q, 2 * BATCH_ROWS * (q + 1))
            base = total([bsr[q, t].astype(F32) for t in range(8)])
            out[r, :] = (base * sd[...] + extra[r]).astype(BF16)

    each(4, chunk)
    for load in loads[6:]:
        load.start()
    relay(0)
    send_far(1)
    send_near(1, 0)
    send_near(1, 1)
    cross_far(0)
    cross_near(0)
    cross_relay(0)
    relay(1)
    cross_end(0)
    local_part(0)
    cross_far(1)
    mix(0)
    cross_near(1)
    spread_start(0)
    cross_relay(1)
    spread_mid(0)
    cross_end(1)
    local_part(1)
    spread_far(0)
    mix(1)
    for c in range(2):
        spread_relay(0, c)
    spread_start(1)
    for c in range(2, 4):
        spread_relay(0, c)
    spread_mid(1)
    for load in loads[6:]:
        load.wait()
    spread_end(0)
    spread_far(1)
    down(0)
    for c in range(4):
        spread_relay(1, c)
    spread_end(1)
    down(1)
    finish()

    for copy in sent:
        copy.wait_send()

    @pl.loop(0, 4)
    def _(k):
        for q in range(BATCHES):
            for m in range(2):
                for s in range(2):
                    for kind in range(3):
                        stage1(q, m, s, kind, k).wait_send()

    for q in range(BATCHES):
        for m in range(2):
            for s in range(2):
                for kind in range(3):
                    stage2(q, m, s, kind).wait_send()


def body(
    tokens, gate_int_codes, up_int_codes, down_int_codes, gate_column_scale, up_column_scale, down_column_scale,
    row_adapter_index, adapter_shrink_weight, adapter_expand_weight,
):
    rows, width = tokens.shape
    cols, wide = down_int_codes.shape
    shrink = jnp.transpose(adapter_shrink_weight, (0, 2, 1)).reshape(-1, cols)
    expand = adapter_expand_weight.reshape(-1, wide)
    by_batch = row_adapter_index.reshape(2, 4, 2, 64).transpose(2, 0, 1, 3).reshape(2, 2, 256)
    by_batch = jnp.pad(by_batch, ((0, 0), (0, 6), (0, 0)))
    by_owner = jnp.pad(row_adapter_index.reshape(8, 128), ((0, 0), (0, 128)))
    ids = jnp.concatenate([by_batch, by_owner[None]], axis=0)[:, :, None, :]
    vmem = pl.BlockSpec(memory_space=pltpu.VMEM)
    hbm = pl.BlockSpec(memory_space=pl.ANY)

    def dma(*shape):
        return [pltpu.SemaphoreType.DMA(shape)] * 2

    n = BATCHES
    return pl.pallas_call(
        layer_kernel,
        out_shape=jax.ShapeDtypeStruct((rows, wide), BF16),
        in_specs=[hbm] * 6 + [vmem] * 4,
        out_specs=vmem,
        scratch_shapes=[
            pltpu.VMEM((4, 4, 64, width), BF16),
            pltpu.VMEM((width, cols), BF16),
            pltpu.VMEM((width, cols), BF16),
            pltpu.VMEM((2, 4, 4, 64, cols), BF16),
            pltpu.VMEM((2, 2, 4, 32, cols), BF16),
            pltpu.VMEM((2, 2, 4, 64, cols), BF16),
            pltpu.VMEM((2, 2, 32, cols), BF16),
            pltpu.VMEM((2, 2, 64, cols), BF16),
            pltpu.VMEM((64, cols), F32),
            pltpu.VMEM((FACTOR, 64, 256), BF16),
            pltpu.VMEM((64, cols), BF16),
            pltpu.VMEM((n, 8, 16, PART_COLS), BF16),
            pltpu.VMEM((n, 8, 16, PART_COLS), BF16),
            pltpu.VMEM((n, 8, 16, PART_COLS), BF16),
            pltpu.VMEM((4, 4, 64, cols), BF16),
            pltpu.VMEM((cols, wide), BF16),
            pltpu.VMEM((16 * ADAPTER_RANK, cols), BF16),
            pltpu.VMEM((256 * ADAPTER_RANK, wide), BF16),
            pltpu.VMEM((n, 8, 2 * BATCH_ROWS, wide), BF16),
            pltpu.VMEM((n, 8, 2 * BATCH_ROWS, wide), BF16),
            pltpu.VMEM((8, ADAPTER_RANK, 128), F32),
            pltpu.VMEM((8, ADAPTER_RANK, 128), F32),
            pltpu.VMEM((4, ADAPTER_RANK, 128), F32),
            pltpu.VMEM((4, ADAPTER_RANK, 128), F32),
            pltpu.SemaphoreType.DMA((9,)),
            *dma(9), *dma(n, 2, 2, 3, 4), *dma(n, 2, 2, 3), *dma(n, 8), *dma(n, 8),
            *dma(n, 2, 2, 2), *dma(n, 2, 2, 2, 4), *dma(n, 8), *dma(8), *dma(2, 4),
        ],
        compiler_params=pltpu.CompilerParams(
            collective_id=0, has_side_effects=True, vmem_limit_bytes=63 * 1024 * 1024
        ),
        name="layer",
    )(
        tokens.reshape(2, 2, 32, width), gate_int_codes, up_int_codes, down_int_codes, shrink, expand,
        gate_column_scale.reshape(1, cols), up_column_scale.reshape(1, cols), down_column_scale.reshape(1, wide), ids,
    )


def solution(mesh):
    return jax.shard_map(
        body,
        mesh=mesh,
        in_specs=(
            P("tensor", "dp"), P("dp", "tensor"), P("dp", "tensor"), P("tensor", "dp"), P("tensor"), P("tensor"),
            P("dp"), P(), P("dp", "tensor", None), P(None, None, "dp"),
        ),
        out_specs=P("tensor", "dp"),
        check_vma=False,
    )
```

time: 381 us -> 160 us (0.42)
  waiting for transfers between devices: 212 us -> 0 us
  Pallas kernels: 93.9 us -> 152 us
  blocking collectives: 24.6 us -> 0 us
  between operations: 13.3 us -> 0.01 us
  local copies, waits for them, and re-layouts: 18 us -> 6.38 us
  matrix products: 9.72 us -> 0 us
  other arithmetic: 6.49 us -> 0.01 us
    psum x1 -> x0, waiting for transfers between devices: 131 us -> none  [body(): shrunk_rows = lax.psum(partial_shrink, ('dp', 'tensor'))]
    pallas_call x1, Pallas kernels: 93.9 us -> 152 us  [body(): pl.pallas_call(layer_kernel, out_shape=jax.ShapeDtypeStruct((rows, wide),...]
    all_gather x1 -> x0, waiting for transfers between devices: 54.4 us -> none  [body(): lax.all_gather(rotated, 'dp', axis=0, tiled=True)]
    unnamed x4 -> x0, waiting for transfers between devices: 26.4 us -> none
    all_to_all x2 -> x0, blocking collectives: 24.6 us -> none  [the longest x1 12.5 us: cross_rotate(): lax.all_to_all(mixed_vals.astype(BF16), 'tensor', split_axis=1, concat_ax...]
    dot_general x2 -> x0, matrix products: 9.72 us -> none  [the longest x1 9.24 us: body(): jnp.dot(lax.all_gather(rotated, 'dp', axis=0, tiled=True), joint_w, prefe...]
  transfers between devices with their start and end apart: 3 -> 0, of which waited for: 3 -> 0; matrix products, arithmetic and copies ran while one was open for 4% -> 0% of each run, Pallas kernels for 0% -> 0%
where the time goes in v2:
time: 160 us; the launch traced here: 159 us
  Pallas kernels  152 us (95%)
  local copies, waits for them, and re-layouts  6.38 us (4%)
    pallas_call x1, Pallas kernels, body(): pl.pallas_call(layer_kernel, out_shape=jax.ShapeDtypeStruct((rows, wide),...  152 us

profile of v2, /device:TPU:1, one launch (start us, length us, event | category | flops | bytes accessed | tf_op | source)
XLA Modules:
  0.0 158.5 jit_solution(9082081854177356197)
XLA Ops:
  0.0 0.7 pad_bitcast_fusion
  0.7 0.8 reshape.33
  1.5 0.1 reshape.34
  1.6 0.6 broadcast_in_dim.7.ids
  2.2 1.3 reshape.30.sg
  3.5 1.3 reshape.31.su
  4.8 152.1 %layer.1 = bf16[128,512]{1,0:T(8,128)(2,1)} custom-call(bf16[2,2,32,512]{3,2,1,0:T(8,128)(2,1)} %bitcast.12, bf16[512,3328]{1,0:T(8,128)(2,1)} %wg_hbm.1, bf16[512,3328]{1,0:T(8,128)(2,1)} %wu_hbm.1, bf16[3328,512]{1,0:T(8,128)(2,1)} %wd_hbm.1, bf16[256,3328]{1,0:T(8,128)(2,1)} %bitcast.11, bf16[4096,512]{1,0:T(8,128)(2,1)} %bitcast.10, ...), custom_call_target="tpu_custom_call" | custom-call | tf_op jit(solution)/shard_map/layer/pallas_call | solution.py:576
  157.0 1.6 copy.13
  (2 shorter events, 0.0 us)

commit v3 on v2

v3 whole, which is shorter than its diff:
```python
import math

import jax
import jax.numpy as jnp
import numpy as np
from jax import lax
from jax.experimental import pallas as pl
from jax.experimental.pallas import tpu as pltpu
from jax.sharding import PartitionSpec as P

FACTOR = 13
ADAPTER_RANK = 16
MESH = pl.DeviceIdType.MESH
F32, BF16 = jnp.float32, jnp.bfloat16


def sylvester_signs(order):
    i = np.arange(order)
    common = i[:, None] & i[None, :]
    parity = np.zeros_like(common)
    while common.any():
        parity ^= common & 1
        common = common >> 1
    return 1 - 2 * parity


def hartley_entries(order):
    i = np.arange(order)
    angle = 2.0 * np.pi * ((i[:, None] * i[None, :]) % order) / order
    return (np.cos(angle) + np.sin(angle)) / math.sqrt(order)


def order_of(j):
    return (2 - j + (j // 2) * (7 - 2 * j)) % 4


BATCHES = 2
BATCH_ROWS = 64 // BATCHES
HALF_ROWS = BATCH_ROWS // 2
PART_SPLIT = 8 // (BATCH_ROWS // 16)
PART_COLS = {2: 1664, 4: 896}[PART_SPLIT]


def part_place(t):
    j = t % PART_SPLIT
    first = 1664 * j if PART_SPLIT == 2 else 128 * (6 * j + (j + 2) // 3)
    return t // PART_SPLIT, first


def each(count, do):
    lax.fori_loop(0, count, lambda i, carry: (do(i), carry)[1], 0)


def layer_kernel(
    tok, wg_hbm, wu_hbm, wd_hbm, shrink_hbm, expand_hbm, sg_hbm, su_hbm, sd_hbm, ids_hbm, out,
    sgv, suv, sdv, ids, scales, xb, wg, wu, p, r1, r2, t1, t2, hid, mid, loc, am, bm, cm, rot, wd, ws, we, bs, bsr, sp, spr, spd,
    load_sem, send_sem, gr, far_r, near_r, t1_r, t2_r, a_r, c_r, g1_r, g1x_r, g2_r, g2x_r, b_r, h_r, d_r,
):
    dp, tensor = lax.axis_index("dp"), lax.axis_index("tensor")
    z, y = dp // 4, dp % 4
    x, core = tensor // 2, tensor % 2
    cols = wg.shape[1]

    def at_x(step, c):
        return (dp, ((x + step) % 4) * 2 + c)

    def at_z(step):
        return (((z + step) % 4) * 4 + y, tensor)

    def at_y(step):
        return (z * 4 + (y + step) % 4, tensor)

    def peer(i):
        return ((x + i // 2) % 4) * 2 + (core + i % 2) % 2

    def before(i):
        return ((x + 4 - i // 2) % 4) * 2 + (core + i % 2) % 2

    far_first = (4, 5, 2, 3, 6, 7, 1)

    pairs = [(tok.at[q, h], xb.at[x, 2 * core + h, pl.ds(32 * q, 32)]) for q in range(2) for h in range(2)]
    pairs += [(wg_hbm, wg), (wu_hbm, wu), (sg_hbm, sgv), (su_hbm, suv), (sd_hbm, sdv), (ids_hbm, ids)]
    pairs += [(wd_hbm, wd), (shrink_hbm, ws), (expand_hbm, we)]
    loads = [pltpu.make_async_copy(a, b, load_sem.at[i]) for i, (a, b) in enumerate(pairs)]
    for load in loads[:10]:
        load.start()

    near = [at_x(i // 2, (core + i % 2) % 2) for i in range(1, 8)]
    others = [(((z + i // 4) % 4) * 4 + (y + i % 4) % 4, tensor) for i in range(1, 16)]
    near += others
    barrier = pltpu.get_barrier_semaphore()
    for who in near:
        pl.semaphore_signal(barrier, inc=1, device_id=who, device_id_type=MESH)
    pl.semaphore_wait(barrier, len(near))

    def remote(src, dst, send, recv, who):
        return pltpu.make_async_remote_copy(
            src_ref=src, dst_ref=dst, send_sem=send, recv_sem=recv, device_id=who, device_id_type=MESH
        )

    mate = at_x(0, 1 - core)
    def shard(q, step, c):
        return xb.at[(x + step) % 4, pl.ds(2 * c, 2), pl.ds(32 * q, 32)]

    def await_bytes(ref, sem):
        remote(ref, ref, send_sem.at[0], sem, mate).wait_recv()

    def gather_copy(q, i, src, dst, who):
        return remote(src, dst, send_sem.at[0 if 0 < i < 4 else 1], gr.at[q, i % 4 if i < 4 else 0], who)

    def gather_start(q):
        for step in (2, 1, 3):
            gather_copy(q, step, tok.at[q], shard(q, 0, core), at_x(step, core)).start()
        gather_copy(q, 0, tok.at[q], shard(q, 0, core), mate).start()

    def gather_mate(q):
        for step in (1, 3, 2):
            ref = shard(q, 4 - step, core)
            await_bytes(ref, gr.at[q, step])
            gather_copy(q, 4, ref, ref, mate).start()

    def gather_end(q):
        await_bytes(xb.at[0], gr.at[q, 0])

    first, second = (z, y), (y, z)
    along = ((at_z, at_y), (at_y, at_z))

    def rows(q, h):
        return pl.ds(pl.multiple_of(BATCH_ROWS * q + HALF_ROWS * h, HALF_ROWS), HALF_ROWS)

    def batch_rows(q):
        return pl.ds(BATCH_ROWS * q, BATCH_ROWS)

    def half_rows(q):
        return pl.ds(HALF_ROWS * q, HALF_ROWS)

    def stage1(q, m, s, kind, k):
        step = 1 + 2 * s
        b = (second[m] + order_of(k)) % 4
        a = (first[m] + (2 if kind == 0 else step)) % 4
        h = 1 - s if kind == 1 else s
        src = p.at[m, a, b, rows(q, h)]
        dst = r1.at[m, s, b, half_rows(q)] if kind == 0 else r2.at[m, s, b, rows(q, h)]
        sem = far_r.at[q, k] if kind == 0 else near_r.at[q, m, k]
        return remote(src, dst, send_sem.at[2], sem, along[m][0](step))

    def stage2(q, m, s, kind):
        step = 1 + 2 * s
        b = (second[m] + (2 if kind == 0 else step)) % 4
        h = 1 - s if kind == 1 else s
        src = p.at[m, first[m], b, rows(q, h)]
        dst = t1.at[m, s, half_rows(q)] if kind == 0 else t2.at[m, s, rows(q, h)]
        sem = t1_r.at[q, s] if kind == 0 else t2_r.at[q]
        return remote(src, dst, send_sem.at[3], sem, along[m][1](step))

    def send_far(q):
        @pl.loop(0, 4)
        def _(k):
            for m in range(2):
                for s in range(2):
                    stage1(q, m, s, 0, k).start()

    def send_near(q, s):
        @pl.loop(0, 4)
        def _(k):
            for m in range(2):
                stage1(q, m, s, 1, k).start()

    def chunk(q, j):
        for m, w in ((0, wg), (1, wu)):
            a = (first[m] + order_of(j)) % 4
            r = batch_rows(q)
            xs = (xb[a, :, r] if m == 0 else xb[:, a, r]).reshape(4 * BATCH_ROWS, xb.shape[-1])
            for n in range(cols // 256):
                block = slice(n * 256, n * 256 + 256)
                v = jnp.dot(xs, w[:, block], preferred_element_type=F32).astype(BF16)
                p[m, a, :, r, block] = v.reshape(4, BATCH_ROWS, 256)

    def first_batch(j):
        chunk(0, j)

        @pl.when(j == 0)
        def _():
            send_far(0)

        @pl.when((j == 1) | (j == 2))
        def _():
            send_near(0, j - 1)

    def second_batch(j):
        chunk(1, j)

    def spread_scales():
        for i in range(cols // 128):
            for m, ref in enumerate((sgv, suv)):
                scales[m, :, i * 128 : i * 128 + 128] = ref[i : i + 1, :]

    def add(dst, *refs):
        def group(i):
            r = pl.ds(pl.multiple_of(i * 16, 16), 16)
            v = dst[r, :].astype(F32)
            for ref in refs:
                v = v + ref[r, :].astype(F32)
            dst[r, :] = v.astype(BF16)

        each(dst.shape[0] // 16, group)

    def relay(q):
        def one(k):
            await_bytes(r1.at[:, :, 0, half_rows(q)], far_r.at[q, k])
            for m in range(2):
                for s in range(2):
                    b = (second[m] + order_of(k)) % 4
                    add(p.at[m, (first[m] + 1 + 2 * s) % 4, b, rows(q, s)], r1.at[m, s, b, half_rows(q)])
                    stage1(q, m, s, 2, k).start()

        each(4, one)

    def settle(q, m, k):
        b = (second[m] + order_of(k)) % 4
        r = batch_rows(q)
        await_bytes(r2.at[m, :, b, r], near_r.at[q, m, k])
        add(p.at[m, first[m], b, r], r2.at[m, 0, b, r], r2.at[m, 1, b, r])

    def cross_far(q):
        for m in range(2):
            settle(q, m, 0)
            for s in range(2):
                stage2(q, m, s, 0).start()

    def cross_near(q):
        for s in range(2):
            for m in range(2):
                settle(q, m, 1 + s)
                stage2(q, m, s, 1).start()

    def cross_relay(q):
        for s in range(2):
            await_bytes(t1.at[:, s, half_rows(q)], t1_r.at[q, s])
            for m in range(2):
                b = (second[m] + 1 + 2 * s) % 4
                add(p.at[m, first[m], b, rows(q, s)], t1.at[m, s, half_rows(q)])
                stage2(q, m, s, 2).start()

    def cross_end(q):
        for m in range(2):
            settle(q, m, 3)
        await_bytes(t2.at[:, :, batch_rows(q)], t2_r.at[q])

    coef = hartley_entries(FACTOR) / math.sqrt(2048)
    lanes = lax.broadcasted_iota(jnp.int32, (256, 256), 0) & lax.broadcasted_iota(jnp.int32, (256, 256), 1)
    for shift in (4, 2, 1):
        lanes = lanes ^ (lanes >> shift)
    signs = (1 - 2 * (lanes & 1)).astype(F32).astype(BF16)

    def local_part(q):
        def gated(i):
            r = pl.ds(pl.multiple_of(BATCH_ROWS * q + i * 16, 16), 16)
            g, u = (
                p[m, first[m], second[m], r, :].astype(F32) + t2[m, 0, r, :].astype(F32) + t2[m, 1, r, :].astype(F32)
                for m in range(2)
            )
            g, u = g * scales[0], u * scales[1]
            hid[r, :] = g / (1.0 + jnp.exp(-g)) * u

        each(BATCH_ROWS // 16, gated)

        def factor(i):
            r = pl.ds(pl.multiple_of(BATCH_ROWS * q + i * 16, 16), 16)
            blocks = [hid[r, a * 256 : a * 256 + 256] for a in range(FACTOR)]
            for b in range(FACTOR):
                v = blocks[0] * float(coef[b, 0])
                for a in range(1, FACTOR):
                    v = v + blocks[a] * float(coef[b, a])
                mid[b, r, :] = v.astype(BF16)

        each(BATCH_ROWS // 16, factor)
        r = batch_rows(q)
        turned = jnp.dot(
            mid[:, r, :].reshape(FACTOR * BATCH_ROWS, 256), signs, preferred_element_type=F32
        ).astype(BF16)
        for b in range(FACTOR):
            loc[r, b * 256 : b * 256 + 256] = turned[b * BATCH_ROWS : (b + 1) * BATCH_ROWS]
        for i in far_first:
            mix_copy(q, i).start()
        am[q, tensor] = my_part(q, tensor)[...]

    def my_part(q, t):
        group, start = part_place(t)
        r = pl.ds(pl.multiple_of(BATCH_ROWS * q + 16 * group, 16), 16)
        return loc.at[r, pl.ds(pl.multiple_of(start, 128), PART_COLS)]

    def mix_copy(q, i):
        to = peer(i)
        return remote(my_part(q, to), am.at[q, tensor], send_sem.at[4], a_r.at[q], (dp, to))

    def back_copy(q, i):
        to = peer(i)
        return remote(bm.at[q, to], cm.at[q, tensor], send_sem.at[5], c_r.at[q], (dp, to))

    def mix(q):
        await_bytes(am.at[q, pl.ds(0, 7)], a_r.at[q])
        for c in range(PART_COLS // 128):
            lane = slice(c * 128, c * 128 + 128)
            v = [am[q, t, :, lane].astype(F32) for t in range(8)]
            for bit in (1, 2, 4):
                v = [v[t] + v[t ^ bit] if t & bit == 0 else v[t ^ bit] - v[t] for t in range(8)]
            for t in range(8):
                bm[q, t, :, lane] = v[t].astype(BF16)
        for i in far_first:
            back_copy(q, i).start()
        cm[q, tensor] = bm[q, tensor]

    def off(c):
        return c + (c // 2) * (5 - 2 * c)

    def held(q, f, c1, c2):
        c = (c1 % 4, c2 % 4) if f == 0 else (c2 % 4, c1 % 4)
        return rot.at[c[0], c[1], rows(q, f)]

    def half_cols(s):
        return pl.ds(s * (cols // 2), cols // 2)

    def spread1(q, f, s, kind):
        step = 1 + 2 * s
        ref = held(q, f, first[f] + (0 if kind == 0 else 4 - step), second[f])
        if kind == 1:
            ref = ref.at[:, half_cols(s)]
        sem = g1_r.at[q, s] if kind == 0 else g1x_r.at[q]
        return remote(ref, ref, send_sem.at[6], sem, along[f][0](step))

    def spread2(q, f, s, kind, c):
        step = 1 + 2 * s
        ref = held(q, f, first[f] + off(c), second[f] + (0 if kind == 0 else 4 - step))
        if kind == 1:
            ref = ref.at[:, half_cols(s)]
        sem = g2_r.at[q, c] if kind == 0 else g2x_r.at[q, c]
        return remote(ref, ref, send_sem.at[7], sem, along[f][1](step))

    def spread_start(q):
        await_bytes(cm.at[q, pl.ds(0, 7)], c_r.at[q])
        for t in range(8):
            group, start = part_place(t)
            r = pl.ds(BATCH_ROWS * q + 16 * group, 16)
            rot[z, y, r, start : start + PART_COLS] = cm[q, t]
        for f in range(2):
            for s in range(2):
                spread1(q, f, s, 0).start()
        for f in range(2):
            for s in range(2):
                spread2(q, f, s, 0, 0).start()

    def spread_mid(q):
        for s in range(2):
            await_bytes(rot.at[0, 0, batch_rows(q)], g1_r.at[q, s])
            for f in range(2):
                spread1(q, f, s, 1).start()
        for s in range(2):
            for f in range(2):
                for s2 in range(2):
                    spread2(q, f, s2, 0, 2 - s).start()

    def spread_far(q):
        await_bytes(rot.at[0, 0, batch_rows(q)], g1x_r.at[q])
        for f in range(2):
            for s2 in range(2):
                spread2(q, f, s2, 0, 3).start()

    def spread_relay(q, c):
        await_bytes(rot.at[0, 0], g2_r.at[q, c])
        for f in range(2):
            for s in range(2):
                spread2(q, f, s, 1, c).start()

    def spread_end(q):
        for c in range(4):
            await_bytes(rot.at[0, 0, batch_rows(q)], g2x_r.at[q, c])

    def sum_piece(q, c1, c2):
        to = 2 * c1 + c2 // 2
        r = pl.ds(pl.multiple_of(BATCH_ROWS * (c2 % 2), BATCH_ROWS), BATCH_ROWS)
        return remote(bs.at[q, to, r], bsr.at[q, tensor, r], send_sem.at[8], b_r.at[q], (dp, to)), to, r

    def ids_of(t):
        row = ids[0:1, :]
        for i in range(1, 8):
            row = jnp.where(t == i, ids[i : i + 1, :], row)
        return row

    lane = lax.broadcasted_iota(jnp.int32, (ADAPTER_RANK, 128), 1)

    def shrink(q, c):
        lhs = rot[c, :, batch_rows(q), :].reshape(4 * BATCH_ROWS, cols)
        parts = lax.dot_general(ws[...], lhs, (((1,), (1,)), ((), ())), preferred_element_type=F32)
        even, odd = 2 * c, 2 * c + 1
        if q == 0:
            id_row = jnp.where(lane[:1] < 64, ids_of(even), pltpu.roll(ids_of(odd), 64, 1))
        else:
            id_row = jnp.where(lane[:1] < 64, pltpu.roll(ids_of(even), 64, 1), ids_of(odd))
        v = jnp.zeros((ADAPTER_RANK, 128), F32)
        for a in range(16):
            v = v + jnp.where(id_row == dp * 16 + a, parts[a * 16 : a * 16 + 16], 0.0)
        turned = pltpu.roll(v, 64, 1)
        if q == 0:
            sp[even] = v
            sp[odd] = turned
        else:
            sp[even] = jnp.where(lane < 64, sp[even], turned)
            sp[odd] = jnp.where(lane < 64, sp[odd], v)

    def shrink_all(q):
        each(4, lambda c: shrink(q, c))

    def shrink_send():
        for i in far_first:
            shrink_copy(i).start()

    def down(q, places):
        places = [((z + i) % 4, (y + j) % 4) for i, j in places]
        lhs = jnp.concatenate([rot[c1, c2, batch_rows(q)] for c1, c2 in places], axis=0)
        base = jnp.dot(lhs, wd[...], preferred_element_type=F32).astype(BF16)
        for n, (c1, c2) in enumerate(places):
            copy, to, r = sum_piece(q, c1, c2)
            bs[q, to, r] = base[n * BATCH_ROWS : (n + 1) * BATCH_ROWS]

            @pl.when(to != tensor)
            def _():
                copy.start()

    def down_early(q):
        for j in (0, 1, 3):
            down(q, [(i, j) for i in (0, 1, 3)])

    def down_late(q):
        down(q, [(2, j) for j in range(4)])
        down(q, [(i, 2) for i in (0, 1, 3)])

    def shrink_copy(i):
        to = peer(i)
        return remote(sp.at[to], spr.at[tensor], send_sem.at[9], h_r.at[0], (dp, to))

    def shrink_across(who):
        return remote(spd.at[dp], spd.at[dp], send_sem.at[10], d_r.at[0], who)

    def total(refs):
        v = refs[0]
        for ref in refs[1:]:
            v = v + ref
        return v

    def finish():
        await_bytes(spr.at[pl.ds(0, 7)], h_r.at[0])
        spr[tensor] = sp[tensor]
        spd[dp] = total([spr[t] for t in range(8)])
        for who in others:
            shrink_across(who).start()
        for q in range(BATCHES):
            await_bytes(bsr.at[q, pl.ds(0, 7)], b_r.at[q])
            bsr[q, tensor] = bs[q, tensor]
        await_bytes(spd.at[pl.ds(0, 15)], d_r.at[0])
        shrunk = total([spd[c] for c in range(16)])
        wide = jnp.concatenate([shrunk] * 8, axis=0).T
        own_ids = jnp.broadcast_to(ids_of(tensor), (128, 128)).astype(F32).T
        lane_adapter = (lax.broadcasted_iota(jnp.int32, (128, 128), 1) // ADAPTER_RANK).astype(F32)
        spot = own_ids - lane_adapter
        chosen = jnp.concatenate(
            [jnp.where(spot == float(8 * j), wide, 0.0).astype(BF16) for j in range(32)], axis=1
        )
        extra = jnp.dot(chosen, we[...], preferred_element_type=F32)
        for q in range(BATCHES):
            r = slice(2 * BATCH_ROWS * q, 2 * BATCH_ROWS * (q + 1))
            base = total([bsr[q, t].astype(F32) for t in range(8)])
            for i in range(out.shape[1] // 128):
                block = slice(i * 128, i * 128 + 128)
                out[r, block] = (base[:, block] * sdv[i : i + 1, :] + extra[r, block]).astype(BF16)

    gather_start(0)
    gather_mate(0)
    for load in loads[:6]:
        load.wait()
    gather_end(0)
    gather_start(1)
    each(4, first_batch)
    gather_mate(1)
    gather_end(1)
    for load in loads[10:]:
        load.start()
    each(4, second_batch)
    for load in loads[6:10]:
        load.wait()
    spread_scales()
    relay(0)
    send_far(1)
    send_near(1, 0)
    send_near(1, 1)
    cross_far(0)
    cross_near(0)
    cross_relay(0)
    relay(1)
    cross_end(0)
    local_part(0)
    cross_far(1)
    mix(0)
    cross_near(1)
    spread_start(0)
    cross_relay(1)
    spread_mid(0)
    cross_end(1)
    local_part(1)
    spread_far(0)
    mix(1)
    for c in range(2):
        spread_relay(0, c)
    spread_start(1)
    for c in range(2, 4):
        spread_relay(0, c)
    spread_mid(1)
    for load in loads[10:]:
        load.wait()
    spread_end(0)
    spread_far(1)
    shrink_all(0)
    down_early(0)
    down_late(0)
    for c in range(4):
        spread_relay(1, c)
    down_early(1)
    spread_end(1)
    shrink_all(1)
    shrink_send()
    down_late(1)
    finish()

    gone = (
        xb.at[pl.ds(0, 2), pl.ds(0, 3)], xb.at[pl.ds(0, 2)], p.at[:, pl.ds(0, 3)], p.at[0, pl.ds(0, 2), pl.ds(0, 3)],
        am.at[:, pl.ds(0, 7)], cm.at[:, pl.ds(0, 7)], rot.at[0, pl.ds(0, 3)], rot.at[pl.ds(0, 3)],
        bs.at[:, pl.ds(0, 7)], sp.at[pl.ds(0, 7)], spd.at[pl.ds(0, 15)],
    )
    for i, ref in enumerate(gone):
        remote(ref, ref, send_sem.at[i], h_r.at[0], mate).wait_send()


def body(
    tokens, gate_int_codes, up_int_codes, down_int_codes, gate_column_scale, up_column_scale, down_column_scale,
    row_adapter_index, adapter_shrink_weight, adapter_expand_weight,
):
    rows, width = tokens.shape
    cols, wide = down_int_codes.shape
    shrink = jnp.transpose(adapter_shrink_weight, (0, 2, 1)).reshape(-1, cols)
    expand = adapter_expand_weight.reshape(-1, wide)
    vmem = pl.BlockSpec(memory_space=pltpu.VMEM)
    hbm = pl.BlockSpec(memory_space=pl.ANY)

    def dma(*shape):
        return pltpu.SemaphoreType.DMA(shape)

    n = BATCHES
    return pl.pallas_call(
        layer_kernel,
        out_shape=jax.ShapeDtypeStruct((rows, wide), BF16),
        in_specs=[hbm] * 10,
        out_specs=vmem,
        scratch_shapes=[
            pltpu.VMEM((cols // 128, 128), F32),
            pltpu.VMEM((cols // 128, 128), F32),
            pltpu.VMEM((wide // 128, 128), F32),
            pltpu.VMEM((8, 128), jnp.int32),
            pltpu.VMEM((2, 1, cols), F32),
            pltpu.VMEM((4, 4, 64, width), BF16),
            pltpu.VMEM((width, cols), BF16),
            pltpu.VMEM((width, cols), BF16),
            pltpu.VMEM((2, 4, 4, 64, cols), BF16),
            pltpu.VMEM((2, 2, 4, 32, cols), BF16),
            pltpu.VMEM((2, 2, 4, 64, cols), BF16),
            pltpu.VMEM((2, 2, 32, cols), BF16),
            pltpu.VMEM((2, 2, 64, cols), BF16),
            pltpu.VMEM((64, cols), F32),
            pltpu.VMEM((FACTOR, 64, 256), BF16),
            pltpu.VMEM((64, cols), BF16),
            pltpu.VMEM((n, 8, 16, PART_COLS), BF16),
            pltpu.VMEM((n, 8, 16, PART_COLS), BF16),
            pltpu.VMEM((n, 8, 16, PART_COLS), BF16),
            pltpu.VMEM((4, 4, 64, cols), BF16),
            pltpu.VMEM((cols, wide), BF16),
            pltpu.VMEM((16 * ADAPTER_RANK, cols), BF16),
            pltpu.VMEM((256 * ADAPTER_RANK, wide), BF16),
            pltpu.VMEM((n, 8, 2 * BATCH_ROWS, wide), BF16),
            pltpu.VMEM((n, 8, 2 * BATCH_ROWS, wide), BF16),
            pltpu.VMEM((8, ADAPTER_RANK, 128), F32),
            pltpu.VMEM((8, ADAPTER_RANK, 128), F32),
            pltpu.VMEM((16, ADAPTER_RANK, 128), F32),
            dma(13), dma(11), dma(n, 4), dma(n, 4), dma(n, 2, 4), dma(n, 2), dma(n), dma(n), dma(n),
            dma(n, 2), dma(n), dma(n, 4), dma(n, 4), dma(n), dma(1), dma(1),
        ],
        compiler_params=pltpu.CompilerParams(
            collective_id=0, has_side_effects=True, vmem_limit_bytes=63 * 1024 * 1024
        ),
        name="layer",
    )(
        tokens.reshape(2, 2, 32, width), gate_int_codes, up_int_codes, down_int_codes, shrink, expand,
        gate_column_scale.reshape(-1, 128), up_column_scale.reshape(-1, 128), down_column_scale.reshape(-1, 128),
        row_adapter_index.reshape(8, 128),
    )


def solution(mesh):
    return jax.shard_map(
        body,
        mesh=mesh,
        in_specs=(
            P("tensor", "dp"), P("dp", "tensor"), P("dp", "tensor"), P("tensor", "dp"), P("tensor"), P("tensor"),
            P("dp"), P(), P("dp", "tensor", None), P(None, None, "dp"),
        ),
        out_specs=P("tensor", "dp"),
        check_vma=False,
    )
```

time: 160 us -> 141 us (0.88)
  Pallas kernels: 152 us -> 139 us
  local copies, waits for them, and re-layouts: 6.38 us -> 1.57 us
    pallas_call x1, Pallas kernels: 152 us -> 139 us  [body(): pl.pallas_call(layer_kernel, out_shape=jax.ShapeDtypeStruct((rows, wide),...]
    reshape x4 -> x0, local copies, waits for them, and re-layouts: 3.49 us -> none  [the longest x1 1.32 us: body(): up_column_scale.reshape(1, cols)]
where the time goes in v3:
time: 141 us; the launch traced here: 140 us
  Pallas kernels  139 us (99%)
  local copies, waits for them, and re-layouts  1.57 us (1%)
    pallas_call x1, Pallas kernels, body(): pl.pallas_call(layer_kernel, out_shape=jax.ShapeDtypeStruct((rows, wide),...  139 us

profile of v3, /device:TPU:1, one launch (start us, length us, event | category | flops | bytes accessed | tf_op | source)
XLA Modules:
  0.0 140.5 jit_solution(6441072534681186373)
XLA Ops:
  0.0 138.9 %layer.1 = bf16[128,512]{1,0:T(8,128)(2,1)} custom-call(bf16[2,2,32,512]{3,2,1,0:T(8,128)(2,1)} %bitcast.11, bf16[512,3328]{1,0:T(8,128)(2,1)} %wg_hbm.1, bf16[512,3328]{1,0:T(8,128)(2,1)} %wu_hbm.1, bf16[3328,512]{1,0:T(8,128)(2,1)} %wd_hbm.1, bf16[256,3328]{1,0:T(8,128)(2,1)} %bitcast.10, bf16[4096,512]{1,0:T(8,128)(2,1)} %bitcast.9, f32[26,128]{1,0:T(8,128)} %bitcast.12, ...), custom_call_target="tpu_custom_call" | custom-call | tf_op jit(solution)/shard_map/layer/pallas_call | solution.py:558
  138.9 1.6 %copy.12 = bf16[128,512]{1,0:T(8,128)(2,1)} copy(bf16[128,512]{1,0:T(8,128)(2,1)} %layer.1) | data formatting | bytes 262144

commit v4 on v3

--- a/solution.py
+++ b/solution.py
@@ -86,7 +86,7 @@
         load.start()
 
     near = [at_x(i // 2, (core + i % 2) % 2) for i in range(1, 8)]
-    others = [(((z + i // 4) % 4) * 4 + (y + i % 4) % 4, tensor) for i in range(1, 16)]
+    others = [(((z + i // 4) % 4) * 4 + (y + i % 4) % 4, tensor) for i in (10, 6, 9, 11, 14, 2, 5, 7, 8, 13, 15, 1, 3, 4, 12)]
     near += others
     barrier = pltpu.get_barrier_semaphore()
     for who in near:
@@ -153,8 +153,8 @@
         sem = t1_r.at[q, s] if kind == 0 else t2_r.at[q]
         return remote(src, dst, send_sem.at[3], sem, along[m][1](step))
 
-    def send_far(q):
-        @pl.loop(0, 4)
+    def send_far(q, low=0, high=4):
+        @pl.loop(low, high)
         def _(k):
             for m in range(2):
                 for s in range(2):
@@ -205,16 +205,13 @@
 
         each(dst.shape[0] // 16, group)
 
-    def relay(q):
-        def one(k):
-            await_bytes(r1.at[:, :, 0, half_rows(q)], far_r.at[q, k])
-            for m in range(2):
-                for s in range(2):
-                    b = (second[m] + order_of(k)) % 4
-                    add(p.at[m, (first[m] + 1 + 2 * s) % 4, b, rows(q, s)], r1.at[m, s, b, half_rows(q)])
-                    stage1(q, m, s, 2, k).start()
-
-        each(4, one)
+    def relay(q, k):
+        await_bytes(r1.at[:, :, 0, half_rows(q)], far_r.at[q, k])
+        for m in range(2):
+            for s in range(2):
+                b = (second[m] + order_of(k)) % 4
+                add(p.at[m, (first[m] + 1 + 2 * s) % 4, b, rows(q, s)], r1.at[m, s, b, half_rows(q)])
+                stage1(q, m, s, 2, k).start()
 
     def settle(q, m, k):
         b = (second[m] + order_of(k)) % 4
@@ -428,12 +425,10 @@
                 copy.start()
 
     def down_early(q):
-        for j in (0, 1, 3):
-            down(q, [(i, j) for i in (0, 1, 3)])
+        down(q, [(i, j) for j in (0, 1, 3) for i in (0, 1, 3)])
 
     def down_late(q):
-        down(q, [(2, j) for j in range(4)])
-        down(q, [(i, 2) for i in (0, 1, 3)])
+        down(q, [(2, j) for j in range(4)] + [(i, 2) for i in (0, 1, 3)])
 
     def shrink_copy(i):
         to = peer(i)
@@ -454,9 +449,11 @@
         spd[dp] = total([spr[t] for t in range(8)])
         for who in others:
             shrink_across(who).start()
+        bases = []
         for q in range(BATCHES):
             await_bytes(bsr.at[q, pl.ds(0, 7)], b_r.at[q])
             bsr[q, tensor] = bs[q, tensor]
+            bases.append(total([bsr[q, t].astype(F32) for t in range(8)]))
         await_bytes(spd.at[pl.ds(0, 15)], d_r.at[0])
         shrunk = total([spd[c] for c in range(16)])
         wide = jnp.concatenate([shrunk] * 8, axis=0).T
@@ -469,7 +466,7 @@
         extra = jnp.dot(chosen, we[...], preferred_element_type=F32)
         for q in range(BATCHES):
             r = slice(2 * BATCH_ROWS * q, 2 * BATCH_ROWS * (q + 1))
-            base = total([bsr[q, t].astype(F32) for t in range(8)])
+            base = bases[q]
             for i in range(out.shape[1] // 128):
                 block = slice(i * 128, i * 128 + 128)
                 out[r, block] = (base[:, block] * sdv[i : i + 1, :] + extra[r, block]).astype(BF16)
@@ -489,41 +486,50 @@
     for load in loads[6:10]:
         load.wait()
     spread_scales()
-    relay(0)
-    send_far(1)
+    send_far(1, 0, 2)
+    relay(0, 0)
+    relay(0, 1)
+    relay(0, 2)
+    relay(0, 3)
+    cross_far(0)
+    cross_near(0)
+    relay(1, 0)
+    relay(1, 1)
+    send_far(1, 2, 4)
+    cross_relay(0)
     send_near(1, 0)
     send_near(1, 1)
-    cross_far(0)
-    cross_near(0)
-    cross_relay(0)
-    relay(1)
+    relay(1, 2)
     cross_end(0)
+    relay(1, 3)
+    cross_far(1)
     local_part(0)
-    cross_far(1)
+    cross_near(1)
     mix(0)
-    cross_near(1)
+    cross_relay(1)
     spread_start(0)
-    cross_relay(1)
-    spread_mid(0)
     cross_end(1)
     local_part(1)
+    spread_mid(0)
+    mix(1)
     spread_far(0)
-    mix(1)
-    for c in range(2):
-        spread_relay(0, c)
+    spread_relay(0, 1)
+    spread_relay(0, 0)
+    spread_relay(0, 2)
     spread_start(1)
-    for c in range(2, 4):
-        spread_relay(0, c)
-    spread_mid(1)
     for load in loads[10:]:
         load.wait()
+    spread_relay(0, 3)
+    spread_mid(1)
+    down_early(0)
     spread_end(0)
     spread_far(1)
     shrink_all(0)
-    down_early(0)
+    spread_relay(1, 1)
     down_late(0)
-    for c in range(4):
-        spread_relay(1, c)
+    spread_relay(1, 2)
+    spread_relay(1, 0)
+    spread_relay(1, 3)
     down_early(1)
     spread_end(1)
     shrink_all(1)

time: 141 us -> 137 us (0.972)
  Pallas kernels: 139 us -> 135 us
    pallas_call x1, Pallas kernels: 139 us -> 135 us  [body(): pl.pallas_call(layer_kernel, out_shape=jax.ShapeDtypeStruct((rows, wide),...]
where the time goes in v4:
time: 137 us; the launch traced here: 136 us
  Pallas kernels  135 us (99%)
  local copies, waits for them, and re-layouts  1.57 us (1%)
    pallas_call x1, Pallas kernels, body(): pl.pallas_call(layer_kernel, out_shape=jax.ShapeDtypeStruct((rows, wide),...  135 us

profile of v4, /device:TPU:1, one launch (start us, length us, event | category | flops | bytes accessed | tf_op | source)
XLA Modules:
  0.0 136.4 jit_solution(6642846123616850377)
XLA Ops:
  0.0 134.8 %layer.1 = bf16[128,512]{1,0:T(8,128)(2,1)} custom-call(bf16[2,2,32,512]{3,2,1,0:T(8,128)(2,1)} %bitcast.11, bf16[512,3328]{1,0:T(8,128)(2,1)} %wg_hbm.1, bf16[512,3328]{1,0:T(8,128)(2,1)} %wu_hbm.1, bf16[3328,512]{1,0:T(8,128)(2,1)} %wd_hbm.1, bf16[256,3328]{1,0:T(8,128)(2,1)} %bitcast.10, bf16[4096,512]{1,0:T(8,128)(2,1)} %bitcast.9, f32[26,128]{1,0:T(8,128)} %bitcast.12, ...), custom_call_target="tpu_custom_call" | custom-call | tf_op jit(solution)/shard_map/layer/pallas_call | solution.py:564
  134.8 1.6 %copy.12 = bf16[128,512]{1,0:T(8,128)(2,1)} copy(bf16[128,512]{1,0:T(8,128)(2,1)} %layer.1) | data formatting | bytes 262144

commit v5 on v4

--- a/solution.py
+++ b/solution.py
@@ -53,7 +53,7 @@
 
 def layer_kernel(
     tok, wg_hbm, wu_hbm, wd_hbm, shrink_hbm, expand_hbm, sg_hbm, su_hbm, sd_hbm, ids_hbm, out,
-    sgv, suv, sdv, ids, scales, xb, wg, wu, p, r1, r2, t1, t2, hid, mid, loc, am, bm, cm, rot, wd, ws, we, bs, bsr, sp, spr, spd,
+    sgv, suv, sdv, ids, scales, signs, xb, wg, wu, p, r1, r2, t1, t2, hid, mid, loc, am, bm, cm, rot, wd, ws, we, bs, bsr, sp, spr, spd,
     load_sem, send_sem, gr, far_r, near_r, t1_r, t2_r, a_r, c_r, g1_r, g1x_r, g2_r, g2x_r, b_r, h_r, d_r,
 ):
     dp, tensor = lax.axis_index("dp"), lax.axis_index("tensor")
@@ -82,15 +82,14 @@
     pairs += [(wg_hbm, wg), (wu_hbm, wu), (sg_hbm, sgv), (su_hbm, suv), (sd_hbm, sdv), (ids_hbm, ids)]
     pairs += [(wd_hbm, wd), (shrink_hbm, ws), (expand_hbm, we)]
     loads = [pltpu.make_async_copy(a, b, load_sem.at[i]) for i, (a, b) in enumerate(pairs)]
-    for load in loads[:10]:
-        load.start()
-
     near = [at_x(i // 2, (core + i % 2) % 2) for i in range(1, 8)]
     others = [(((z + i // 4) % 4) * 4 + (y + i % 4) % 4, tensor) for i in (10, 6, 9, 11, 14, 2, 5, 7, 8, 13, 15, 1, 3, 4, 12)]
     near += others
     barrier = pltpu.get_barrier_semaphore()
     for who in near:
         pl.semaphore_signal(barrier, inc=1, device_id=who, device_id_type=MESH)
+    for load in loads[:10]:
+        load.start()
     pl.semaphore_wait(barrier, len(near))
 
     def remote(src, dst, send, recv, who):
@@ -191,6 +190,10 @@
         chunk(1, j)
 
     def spread_scales():
+        lanes = lax.broadcasted_iota(jnp.int32, (256, 256), 0) & lax.broadcasted_iota(jnp.int32, (256, 256), 1)
+        for shift in (4, 2, 1):
+            lanes = lanes ^ (lanes >> shift)
+        signs[...] = (1 - 2 * (lanes & 1)).astype(F32).astype(BF16)
         for i in range(cols // 128):
             for m, ref in enumerate((sgv, suv)):
                 scales[m, :, i * 128 : i * 128 + 128] = ref[i : i + 1, :]
@@ -245,11 +248,6 @@
         await_bytes(t2.at[:, :, batch_rows(q)], t2_r.at[q])
 
     coef = hartley_entries(FACTOR) / math.sqrt(2048)
-    lanes = lax.broadcasted_iota(jnp.int32, (256, 256), 0) & lax.broadcasted_iota(jnp.int32, (256, 256), 1)
-    for shift in (4, 2, 1):
-        lanes = lanes ^ (lanes >> shift)
-    signs = (1 - 2 * (lanes & 1)).astype(F32).astype(BF16)
-
     def local_part(q):
         def gated(i):
             r = pl.ds(pl.multiple_of(BATCH_ROWS * q + i * 16, 16), 16)
@@ -274,7 +272,7 @@
         each(BATCH_ROWS // 16, factor)
         r = batch_rows(q)
         turned = jnp.dot(
-            mid[:, r, :].reshape(FACTOR * BATCH_ROWS, 256), signs, preferred_element_type=F32
+            mid[:, r, :].reshape(FACTOR * BATCH_ROWS, 256), signs[...], preferred_element_type=F32
         ).astype(BF16)
         for b in range(FACTOR):
             loc[r, b * 256 : b * 256 + 256] = turned[b * BATCH_ROWS : (b + 1) * BATCH_ROWS]
@@ -386,27 +384,30 @@
 
     lane = lax.broadcasted_iota(jnp.int32, (ADAPTER_RANK, 128), 1)
 
-    def shrink(q, c):
-        lhs = rot[c, :, batch_rows(q), :].reshape(4 * BATCH_ROWS, cols)
-        parts = lax.dot_general(ws[...], lhs, (((1,), (1,)), ((), ())), preferred_element_type=F32)
-        even, odd = 2 * c, 2 * c + 1
-        if q == 0:
-            id_row = jnp.where(lane[:1] < 64, ids_of(even), pltpu.roll(ids_of(odd), 64, 1))
-        else:
-            id_row = jnp.where(lane[:1] < 64, pltpu.roll(ids_of(even), 64, 1), ids_of(odd))
-        v = jnp.zeros((ADAPTER_RANK, 128), F32)
-        for a in range(16):
-            v = v + jnp.where(id_row == dp * 16 + a, parts[a * 16 : a * 16 + 16], 0.0)
-        turned = pltpu.roll(v, 64, 1)
-        if q == 0:
-            sp[even] = v
-            sp[odd] = turned
-        else:
-            sp[even] = jnp.where(lane < 64, sp[even], turned)
-            sp[odd] = jnp.where(lane < 64, sp[odd], v)
+    def shrink(q, g):
+        lhs = rot[pl.ds(2 * g, 2), :, batch_rows(q), :].reshape(8 * BATCH_ROWS, cols)
+        both = lax.dot_general(ws[...], lhs, (((1,), (1,)), ((), ())), preferred_element_type=F32)
+        for i in range(2):
+            parts = both[:, i * 128 : i * 128 + 128]
+            even, odd = 4 * g + 2 * i, 4 * g + 2 * i + 1
+            if q == 0:
+                id_row = jnp.where(lane[:1] < 64, ids_of(even), pltpu.roll(ids_of(odd), 64, 1))
+            else:
+                id_row = jnp.where(lane[:1] < 64, pltpu.roll(ids_of(even), 64, 1), ids_of(odd))
+            v = jnp.zeros((ADAPTER_RANK, 128), F32)
+            for a in range(16):
+                v = v + jnp.where(id_row == dp * 16 + a, parts[a * 16 : a * 16 + 16], 0.0)
+            turned = pltpu.roll(v, 64, 1)
+            if q == 0:
+                sp[even] = v
+                sp[odd] = turned
+            else:
+                sp[even] = jnp.where(lane < 64, sp[even], turned)
+                sp[odd] = jnp.where(lane < 64, sp[odd], v)
 
     def shrink_all(q):
-        each(4, lambda c: shrink(q, c))
+        for g in range(2):
+            shrink(q, g)
 
     def shrink_send():
         for i in far_first:
@@ -563,7 +564,7 @@
     n = BATCHES
     return pl.pallas_call(
         layer_kernel,
-        out_shape=jax.ShapeDtypeStruct((rows, wide), BF16),
+        out_shape=pltpu.VMEM((rows, wide), BF16),
         in_specs=[hbm] * 10,
         out_specs=vmem,
         scratch_shapes=[
@@ -572,6 +573,7 @@
             pltpu.VMEM((wide // 128, 128), F32),
             pltpu.VMEM((8, 128), jnp.int32),
             pltpu.VMEM((2, 1, cols), F32),
+            pltpu.VMEM((256, 256), BF16),
             pltpu.VMEM((4, 4, 64, width), BF16),
             pltpu.VMEM((width, cols), BF16),
             pltpu.VMEM((width, cols), BF16),

time: 137 us -> 133 us (0.971)
  Pallas kernels: 135 us -> 133 us
    pallas_call x1, Pallas kernels: 135 us -> 133 us  [body(): pl.pallas_call(layer_kernel, out_shape=pltpu.VMEM((rows, wide), BF16), in...]
where the time goes in v5:
time: 133 us
  Pallas kernels  133 us (100%)
    pallas_call x1, Pallas kernels, body(): pl.pallas_call(layer_kernel, out_shape=pltpu.VMEM((rows, wide), BF16), in...  133 us

profile of v5, /device:TPU:1, one launch (start us, length us, event | category | flops | bytes accessed | tf_op | source)
XLA Modules:
  0.0 133.3 jit_solution(1180117676839470888)
XLA Ops:
  0.0 132.6 %layer.1 = bf16[128,512]{1,0:T(8,128)(2,1)S(1)} custom-call(bf16[2,2,32,512]{3,2,1,0:T(8,128)(2,1)} %bitcast.11, bf16[512,3328]{1,0:T(8,128)(2,1)} %wg_hbm.1, bf16[512,3328]{1,0:T(8,128)(2,1)} %wu_hbm.1, bf16[3328,512]{1,0:T(8,128)(2,1)} %wd_hbm.1, bf16[256,3328]{1,0:T(8,128)(2,1)} %bitcast.10, bf16[4096,512]{1,0:T(8,128)(2,1)} %bitcast.9, ...), custom_call_target="tpu_custom_call" | custom-call | tf_op jit(solution)/shard_map/layer/pallas_call | solution.py:565
  132.6 0.7 copy.12

commit v6 on v5

--- a/solution.py
+++ b/solution.py
@@ -53,7 +53,7 @@
 
 def layer_kernel(
     tok, wg_hbm, wu_hbm, wd_hbm, shrink_hbm, expand_hbm, sg_hbm, su_hbm, sd_hbm, ids_hbm, out,
-    sgv, suv, sdv, ids, scales, signs, xb, wg, wu, p, r1, r2, t1, t2, hid, mid, loc, am, bm, cm, rot, wd, ws, we, bs, bsr, sp, spr, spd,
+    sgv, suv, sdv, ids, scales, signs, owner, xb, wg, wu, p, r1, r2, t1, t2, hid, mid, loc, am, bm, cm, rot, wd, ws, we, bs, bsr, sp, spr, spd,
     load_sem, send_sem, gr, far_r, near_r, t1_r, t2_r, a_r, c_r, g1_r, g1x_r, g2_r, g2x_r, b_r, h_r, d_r,
 ):
     dp, tensor = lax.axis_index("dp"), lax.axis_index("tensor")
@@ -188,6 +188,13 @@
 
     def second_batch(j):
         chunk(1, j)
+
+    def mark_owners():
+        own_ids = jnp.broadcast_to(ids_of(tensor), (128, 128)).astype(F32).T
+        lane_adapter = (lax.broadcasted_iota(jnp.int32, (128, 128), 1) // ADAPTER_RANK).astype(F32)
+        spot = own_ids - lane_adapter
+        for j in range(32):
+            owner[:, j * 128 : j * 128 + 128] = jnp.where(spot == float(8 * j), 1.0, 0.0).astype(BF16)
 
     def spread_scales():
         lanes = lax.broadcasted_iota(jnp.int32, (256, 256), 0) & lax.broadcasted_iota(jnp.int32, (256, 256), 1)
@@ -458,12 +465,7 @@
         await_bytes(spd.at[pl.ds(0, 15)], d_r.at[0])
         shrunk = total([spd[c] for c in range(16)])
         wide = jnp.concatenate([shrunk] * 8, axis=0).T
-        own_ids = jnp.broadcast_to(ids_of(tensor), (128, 128)).astype(F32).T
-        lane_adapter = (lax.broadcasted_iota(jnp.int32, (128, 128), 1) // ADAPTER_RANK).astype(F32)
-        spot = own_ids - lane_adapter
-        chosen = jnp.concatenate(
-            [jnp.where(spot == float(8 * j), wide, 0.0).astype(BF16) for j in range(32)], axis=1
-        )
+        chosen = owner[...] * jnp.concatenate([wide.astype(BF16)] * 32, axis=1)
         extra = jnp.dot(chosen, we[...], preferred_element_type=F32)
         for q in range(BATCHES):
             r = slice(2 * BATCH_ROWS * q, 2 * BATCH_ROWS * (q + 1))
@@ -518,6 +520,7 @@
     spread_relay(0, 0)
     spread_relay(0, 2)
     spread_start(1)
+    mark_owners()
     for load in loads[10:]:
         load.wait()
     spread_relay(0, 3)
@@ -574,6 +577,7 @@
             pltpu.VMEM((8, 128), jnp.int32),
             pltpu.VMEM((2, 1, cols), F32),
             pltpu.VMEM((256, 256), BF16),
+            pltpu.VMEM((128, 256 * ADAPTER_RANK), BF16),
             pltpu.VMEM((4, 4, 64, width), BF16),
             pltpu.VMEM((width, cols), BF16),
             pltpu.VMEM((width, cols), BF16),

time: 133 us -> 133 us (level)
  no operation moved by 1% of the time
where the time goes in v6:
time: 133 us
  Pallas kernels  133 us (100%)
    pallas_call x1, Pallas kernels, body(): pl.pallas_call(layer_kernel, out_shape=pltpu.VMEM((rows, wide), BF16), in...  133 us

profile of v6, /device:TPU:1, one launch (start us, length us, event | category | flops | bytes accessed | tf_op | source)
XLA Modules:
  0.0 133.3 jit_solution(6561708861976988075)
XLA Ops:
  0.0 132.6 %layer.1 = bf16[128,512]{1,0:T(8,128)(2,1)S(1)} custom-call(bf16[2,2,32,512]{3,2,1,0:T(8,128)(2,1)} %bitcast.11, bf16[512,3328]{1,0:T(8,128)(2,1)} %wg_hbm.1, bf16[512,3328]{1,0:T(8,128)(2,1)} %wu_hbm.1, bf16[3328,512]{1,0:T(8,128)(2,1)} %wd_hbm.1, bf16[256,3328]{1,0:T(8,128)(2,1)} %bitcast.10, bf16[4096,512]{1,0:T(8,128)(2,1)} %bitcast.9, ...), custom_call_target="tpu_custom_call" | custom-call | tf_op jit(solution)/shard_map/layer/pallas_call | solution.py:568
  132.6 0.7 copy.12
